TPU v7x, 32 devices: a whole 2x2x4 slice. The times are simulated.
32 devices in a mesh: item: 2 (over x), lat: 4 (over y, core), pix: 4 (over z).
Axes of the slice: x: 2, y: 2, z: 4, core: 2. Of those that a mesh axis runs over, the one named last changes fastest.
Arguments:
- latents: bfloat16 [8, 512, 1024], P('item', ('lat', 'pix')), may hold values from -6 to 6
- pixels: bfloat16 [8, 32768, 261], P('item', ('lat', 'pix')), may hold values from -6 to 6
- size_ids: int32 [8], P('item'), may hold values from 0 to 2, as said below
- cross_gain: float32 [1024], replicated, may hold values from 0.25 to 1.75
- pixel_gain: float32 [261], replicated, may hold values from 0.25 to 1.75
- query_weight: bfloat16 [1024, 1024], replicated, may hold values from -0.1875 to 0.1875
- key_weight: bfloat16 [261, 1024], replicated, may hold values from -0.375 to 0.375
- value_weight: bfloat16 [261, 1024], replicated, may hold values from -0.375 to 0.375
- cross_output: bfloat16 [1024, 1024], replicated, may hold values from -9 to 9
- first_gain: float32 [1024], replicated, may hold values from 0.25 to 1.75
- first_up: bfloat16 [1024, 1024], replicated, may hold values from -0.1875 to 0.1875
- first_down: bfloat16 [1024, 1024], replicated, may hold values from -0.1875 to 0.1875
- self_gain: float32 [1024], replicated, may hold values from 0.25 to 1.75
- self_inputs: bfloat16 [1024, 3072], replicated, may hold values from -0.1875 to 0.1875
- self_output: bfloat16 [1024, 1024], replicated, may hold values from -2.5 to 2.5
- second_gain: float32 [1024], replicated, may hold values from 0.25 to 1.75
- second_up: bfloat16 [1024, 1024], replicated, may hold values from -0.1875 to 0.1875
- second_down: bfloat16 [1024, 1024], replicated, may hold values from -0.1875 to 0.1875
- cotangent: bfloat16 [8, 512, 1024], P('item', ('lat', 'pix')), may hold values from -6 to 6
Outputs:
- latents_out: bfloat16 [8, 512, 1024], P('item', ('lat', 'pix'))
- latent_grad: bfloat16 [8, 512, 1024], P('item', ('lat', 'pix'))
- pixel_grad: bfloat16 [8, 32768, 261], P('item', ('lat', 'pix'))
- query_grad: float32 [1024, 1024], P(('item', 'lat', 'pix'))
- cross_out_grad: float32 [1024, 1024], P(('item', 'lat', 'pix'))
- first_up_grad: float32 [1024, 1024], P(('item', 'lat', 'pix'))
- first_down_grad: float32 [1024, 1024], P(('item', 'lat', 'pix'))
- self_in_grad: float32 [1024, 3072], P(('item', 'lat', 'pix'))
- self_out_grad: float32 [1024, 1024], P(('item', 'lat', 'pix'))
- second_up_grad: float32 [1024, 1024], P(('item', 'lat', 'pix'))
- second_down_grad: float32 [1024, 1024], P(('item', 'lat', 'pix'))
- key_grad: float32 [261, 1024], replicated
- value_grad: float32 [261, 1024], replicated
- cross_gain_grad: float32 [1024], replicated
- pixel_gain_grad: float32 [261], replicated
- first_gain_grad: float32 [1024], replicated
- self_gain_grad: float32 [1024], replicated
- second_gain_grad: float32 [1024], replicated
Inputs may be any that keep to these rules, and one draw needn't show every extreme that they name: `size_ids`: each of the sizes 0, 1 and 2 is given to at least one image.
All inputs are finite; a program needn't handle non-finite values.
Results may differ from a plain program's by a relative error of at most 0.025.
Values may be sent and summed in bfloat16 or wider, within the bound.
No kernel may reach another device: no remote copies, remote signals or barrier semaphores. Data moves between devices by JAX's collectives and lax.ppermute only.
A program may use at most 256 MiB of HBM per device.

v0:
```python
import math

import jax
import jax.numpy as jnp
from jax import lax
from jax.sharding import PartitionSpec as P

HEADS = 8


epsilon = 1e-05


def norm_rows(inputs, gain):
    centred = inputs - jnp.mean(inputs, axis=-1, keepdims=True)
    inverse = lax.rsqrt(jnp.mean(centred * centred, axis=-1, keepdims=True) + epsilon)
    normed = centred * inverse
    return (normed * gain, normed, inverse)


def norm_back(upstream, normed, inverse, gain):
    scaled = upstream * gain
    first_mean = jnp.mean(scaled, axis=-1, keepdims=True)
    second_mean = jnp.mean(scaled * normed, axis=-1, keepdims=True)
    return inverse * (scaled - first_mean - normed * second_mean)


def activation(inputs):
    return jax.nn.gelu(inputs, approximate=True)


def forward_mat(left, right):
    return jnp.dot(left, right, preferred_element_type=jnp.float32)


def left_mat(left, right):
    return jnp.einsum("rk,rd->kd", left, right, preferred_element_type=jnp.float32)


def right_mat(left, right):
    return jnp.einsum("rd,kd->rk", left, right, preferred_element_type=jnp.float32)


def feed_forward(residual, gain, up_weight, down_weight):
    normed_full, normed, inverse = norm_rows(residual, gain)
    rounded_in = normed_full.astype(jnp.bfloat16)
    hidden = forward_mat(rounded_in, up_weight)
    active = activation(hidden).astype(jnp.bfloat16)
    return (
        residual + forward_mat(active, down_weight),
        (rounded_in, normed, inverse, hidden, active),
    )


def feed_back(upstream, kept, gain, up_weight, down_weight):
    rounded_in, normed, inverse, hidden, active = kept
    sent = upstream.astype(jnp.bfloat16)
    down_grad = left_mat(active, sent)
    unused, gelu_pull = jax.vjp(activation, hidden)
    hidden_grad = gelu_pull(right_mat(sent, down_weight))[0].astype(jnp.bfloat16)
    up_grad = left_mat(rounded_in, hidden_grad)
    normed_grad = right_mat(hidden_grad, up_weight)
    gain_grad = jnp.sum(normed_grad * normed, axis=0)
    return (upstream + norm_back(normed_grad, normed, inverse, gain), up_grad, down_grad, gain_grad)


def body(
    latents,
    pixels,
    size_ids,
    cross_gain,
    pixel_gain,
    query_weight,
    key_weight,
    value_weight,
    cross_output,
    first_gain,
    first_up,
    first_down,
    self_gain,
    self_inputs,
    self_output,
    second_gain,
    second_up,
    second_down,
    cotangent,
):
    images, lat_rows, width = latents.shape
    pix_rows = pixels.shape[1]
    head_dim = width // HEADS
    group = lax.axis_size(("lat", "pix"))
    block = lax.axis_index(("lat", "pix"))
    all_rows = lat_rows * group
    rows = images * lat_rows
    scale = 1.0 / math.sqrt(width)
    head_scale = 1.0 / math.sqrt(head_dim)
    factor = jnp.where(size_ids == 0, 25, jnp.where(size_ids == 1, 49, 81)).astype(jnp.int32)
    counts = pix_rows * group * factor // 81
    positions = block * pix_rows + jnp.arange(pix_rows, dtype=jnp.int32)
    valid = positions[None, :] < counts[:, None]
    residual_zero = latents.astype(jnp.float32).reshape(rows, width)
    normed_full, normed_one, inverse_one = norm_rows(residual_zero, cross_gain)
    rounded_one = normed_full.astype(jnp.bfloat16)
    query_own = (
        forward_mat(rounded_one, query_weight).astype(jnp.bfloat16).reshape(images, lat_rows, width)
    )
    query_all = lax.all_gather(query_own, ("lat", "pix"), axis=1, tiled=True)
    pixel_full, pixel_normed, pixel_inverse = norm_rows(pixels.astype(jnp.float32), pixel_gain)
    pixel_rounded = pixel_full.astype(jnp.bfloat16)
    pixel_keys = jnp.einsum(
        "ipc,cd->ipd", pixel_rounded, key_weight, preferred_element_type=jnp.float32
    ).astype(jnp.bfloat16)
    pixel_values = jnp.einsum(
        "ipc,cd->ipd", pixel_rounded, value_weight, preferred_element_type=jnp.float32
    ).astype(jnp.bfloat16)
    scores = (
        jnp.einsum("ild,ipd->ilp", query_all, pixel_keys, preferred_element_type=jnp.float32)
        * scale
    )
    powered = jnp.where(valid[:, None, :], jnp.exp(scores), 0.0)
    powered_low = powered.astype(jnp.bfloat16)
    totals = jnp.sum(powered, axis=2)
    numerator = jnp.einsum(
        "ilp,ipd->ild", powered_low, pixel_values, preferred_element_type=jnp.float32
    )
    numer_all, totals_all = (
        lax.psum(numerator.astype(jnp.bfloat16), ("lat", "pix")).astype(jnp.float32),
        lax.psum(totals.astype(jnp.bfloat16), ("lat", "pix")).astype(jnp.float32),
    )
    start = block * lat_rows
    numer_own = lax.dynamic_slice_in_dim(numer_all, start, lat_rows, 1)
    totals_own = lax.dynamic_slice_in_dim(totals_all, start, lat_rows, 1)
    attended = numer_own / totals_own[:, :, None]
    cross_mixed = attended.astype(jnp.bfloat16).reshape(rows, width)
    residual_one = residual_zero + forward_mat(cross_mixed, cross_output)
    residual_two, first_kept = feed_forward(residual_one, first_gain, first_up, first_down)
    normed_full, normed_three, inverse_three = norm_rows(residual_two, self_gain)
    rounded_three = normed_full.astype(jnp.bfloat16)
    projected = (
        forward_mat(rounded_three, self_inputs)
        .astype(jnp.bfloat16)
        .reshape(images, lat_rows, 3 * width)
    )
    pair_all = lax.all_gather(projected[:, :, width:], ("lat", "pix"), axis=1, tiled=True)
    self_query = projected[:, :, :width].reshape(images, lat_rows, HEADS, head_dim)
    self_keys = pair_all[:, :, :width].reshape(images, all_rows, HEADS, head_dim)
    self_values = pair_all[:, :, width:].reshape(images, all_rows, HEADS, head_dim)
    self_scores = (
        jnp.einsum("ilhe,imhe->ihlm", self_query, self_keys, preferred_element_type=jnp.float32)
        * head_scale
    )
    self_powered = jnp.exp(self_scores)
    self_low = self_powered.astype(jnp.bfloat16)
    self_totals = jnp.transpose(jnp.sum(self_powered, axis=3), (0, 2, 1))
    self_numerator = jnp.einsum(
        "ihlm,imhe->ilhe", self_low, self_values, preferred_element_type=jnp.float32
    )
    self_mixed = self_numerator / self_totals[..., None]
    self_rounded = self_mixed.astype(jnp.bfloat16).reshape(rows, width)
    residual_three = residual_two + forward_mat(self_rounded, self_output)
    output_rows, second_kept = feed_forward(residual_three, second_gain, second_up, second_down)
    latents_out = output_rows.astype(jnp.bfloat16).reshape(images, lat_rows, width)
    upstream = cotangent.astype(jnp.float32).reshape(rows, width)
    back_three, second_up_grad, second_down_grad, second_gain_grad = feed_back(
        upstream, second_kept, second_gain, second_up, second_down
    )
    sent_three = back_three.astype(jnp.bfloat16)
    self_out_grad = left_mat(self_rounded, sent_three)
    mixed_grad = (
        right_mat(sent_three, self_output)
        .astype(jnp.bfloat16)
        .reshape(images, lat_rows, HEADS, head_dim)
    )
    mixed_wide = mixed_grad.astype(jnp.float32)
    numer_grad = (mixed_wide / self_totals[..., None]).astype(jnp.bfloat16)
    total_grad = -jnp.sum(mixed_wide * self_mixed, axis=3) / self_totals
    power_grad = jnp.einsum(
        "ilhe,imhe->ihlm", numer_grad, self_values, preferred_element_type=jnp.float32
    )
    score_grad = (
        self_powered * (power_grad + jnp.transpose(total_grad, (0, 2, 1))[..., None])
    ).astype(jnp.bfloat16)
    query_part = (
        jnp.einsum("ihlm,imhe->ilhe", score_grad, self_keys, preferred_element_type=jnp.float32)
        * head_scale
    )
    key_part = (
        jnp.einsum("ihlm,ilhe->imhe", score_grad, self_query, preferred_element_type=jnp.float32)
        * head_scale
    )
    value_part = jnp.einsum(
        "ihlm,ilhe->imhe", self_low, numer_grad, preferred_element_type=jnp.float32
    )
    pair_grad = jnp.concatenate(
        [key_part.reshape(images, all_rows, width), value_part.reshape(images, all_rows, width)],
        axis=2,
    )
    pair_own = lax.psum_scatter(
        pair_grad.astype(jnp.bfloat16), ("lat", "pix"), scatter_dimension=1, tiled=True
    ).astype(jnp.float32)
    projected_grad = (
        jnp.concatenate([query_part.reshape(images, lat_rows, width), pair_own], axis=2)
        .astype(jnp.bfloat16)
        .reshape(rows, 3 * width)
    )
    self_in_grad = left_mat(rounded_three, projected_grad)
    normed_grad = right_mat(projected_grad, self_inputs)
    self_gain_grad = jnp.sum(normed_grad * normed_three, axis=0)
    back_two = back_three + norm_back(normed_grad, normed_three, inverse_three, self_gain)
    back_one, first_up_grad, first_down_grad, first_gain_grad = feed_back(
        back_two, first_kept, first_gain, first_up, first_down
    )
    sent_one = back_one.astype(jnp.bfloat16)
    cross_out_grad = left_mat(cross_mixed, sent_one)
    attended_grad = right_mat(sent_one, cross_output).astype(jnp.bfloat16).astype(jnp.float32)
    attended_grad = attended_grad.reshape(images, lat_rows, width)
    numer_own_grad = (attended_grad / totals_own[:, :, None]).astype(jnp.bfloat16)
    totals_own_grad = -jnp.sum(attended_grad * attended, axis=2) / totals_own
    numer_grad_all, totals_grad_all = (
        lax.all_gather(numer_own_grad, ("lat", "pix"), axis=1, tiled=True),
        lax.all_gather(
            totals_own_grad.astype(jnp.bfloat16), ("lat", "pix"), axis=1, tiled=True
        ).astype(totals_own_grad.dtype),
    )
    cross_power_grad = jnp.einsum(
        "ild,ipd->ilp", numer_grad_all, pixel_values, preferred_element_type=jnp.float32
    )
    cross_score_grad = (powered * (cross_power_grad + totals_grad_all[:, :, None])).astype(
        jnp.bfloat16
    )
    query_part_cross = (
        jnp.einsum("ilp,ipd->ild", cross_score_grad, pixel_keys, preferred_element_type=jnp.float32)
        * scale
    )
    query_rows_grad = lax.psum_scatter(
        query_part_cross.astype(jnp.bfloat16), ("lat", "pix"), scatter_dimension=1, tiled=True
    ).astype(jnp.float32)
    query_rows_grad = query_rows_grad.astype(jnp.bfloat16).reshape(rows, width)
    key_rows_grad = (
        jnp.einsum("ilp,ild->ipd", cross_score_grad, query_all, preferred_element_type=jnp.float32)
        * scale
    ).astype(jnp.bfloat16)
    value_rows_grad = jnp.einsum(
        "ilp,ild->ipd", powered_low, numer_grad_all, preferred_element_type=jnp.float32
    ).astype(jnp.bfloat16)
    pixel_normed_grad = jnp.einsum(
        "ipd,cd->ipc", key_rows_grad, key_weight, preferred_element_type=jnp.float32
    ) + jnp.einsum("ipd,cd->ipc", value_rows_grad, value_weight, preferred_element_type=jnp.float32)
    key_grad = jnp.einsum(
        "ipc,ipd->cd", pixel_rounded, key_rows_grad, preferred_element_type=jnp.float32
    )
    value_grad = jnp.einsum(
        "ipc,ipd->cd", pixel_rounded, value_rows_grad, preferred_element_type=jnp.float32
    )
    pixel_gain_grad = jnp.sum(pixel_normed_grad * pixel_normed, axis=(0, 1))
    pixel_grad = norm_back(pixel_normed_grad, pixel_normed, pixel_inverse, pixel_gain).astype(
        jnp.bfloat16
    )
    query_grad = left_mat(rounded_one, query_rows_grad)
    normed_one_grad = right_mat(query_rows_grad, query_weight)
    cross_gain_grad = jnp.sum(normed_one_grad * normed_one, axis=0)
    latent_grad = back_one + norm_back(normed_one_grad, normed_one, inverse_one, cross_gain)
    latent_grad = latent_grad.astype(jnp.bfloat16).reshape(images, lat_rows, width)
    (
        query_grad,
        cross_out_grad,
        first_up_grad,
        first_down_grad,
        self_in_grad,
        self_out_grad,
        second_up_grad,
        second_down_grad,
    ) = (
        lax.psum_scatter(query_grad, ("item", "lat", "pix"), scatter_dimension=0, tiled=True),
        lax.psum_scatter(cross_out_grad, ("item", "lat", "pix"), scatter_dimension=0, tiled=True),
        lax.psum_scatter(first_up_grad, ("item", "lat", "pix"), scatter_dimension=0, tiled=True),
        lax.psum_scatter(first_down_grad, ("item", "lat", "pix"), scatter_dimension=0, tiled=True),
        lax.psum_scatter(self_in_grad, ("item", "lat", "pix"), scatter_dimension=0, tiled=True),
        lax.psum_scatter(self_out_grad, ("item", "lat", "pix"), scatter_dimension=0, tiled=True),
        lax.psum_scatter(second_up_grad, ("item", "lat", "pix"), scatter_dimension=0, tiled=True),
        lax.psum_scatter(second_down_grad, ("item", "lat", "pix"), scatter_dimension=0, tiled=True),
    )
    (
        key_grad,
        value_grad,
        cross_gain_grad,
        pixel_gain_grad,
        first_gain_grad,
        self_gain_grad,
        second_gain_grad,
    ) = lax.psum(
        (
            key_grad,
            value_grad,
            cross_gain_grad,
            pixel_gain_grad,
            first_gain_grad,
            self_gain_grad,
            second_gain_grad,
        ),
        ("item", "lat", "pix"),
    )
    return (
        latents_out,
        latent_grad,
        pixel_grad,
        query_grad,
        cross_out_grad,
        first_up_grad,
        first_down_grad,
        self_in_grad,
        self_out_grad,
        second_up_grad,
        second_down_grad,
        key_grad,
        value_grad,
        cross_gain_grad,
        pixel_gain_grad,
        first_gain_grad,
        self_gain_grad,
        second_gain_grad,
    )


def solution(mesh):
    in_specs = (
        P("item", ("lat", "pix"), None),
        P("item", ("lat", "pix"), None),
        P("item"),
        P(),
        P(),
        P(),
        P(),
        P(),
        P(),
        P(),
        P(),
        P(),
        P(),
        P(),
        P(),
        P(),
        P(),
        P(),
        P("item", ("lat", "pix"), None),
    )
    out_specs = (
        P("item", ("lat", "pix"), None),
        P("item", ("lat", "pix"), None),
        P("item", ("lat", "pix"), None),
        P(("item", "lat", "pix"), None),
        P(("item", "lat", "pix"), None),
        P(("item", "lat", "pix"), None),
        P(("item", "lat", "pix"), None),
        P(("item", "lat", "pix"), None),
        P(("item", "lat", "pix"), None),
        P(("item", "lat", "pix"), None),
        P(("item", "lat", "pix"), None),
        P(),
        P(),
        P(),
        P(),
        P(),
        P(),
        P(),
    )
    return jax.shard_map(body, mesh=mesh, in_specs=in_specs, out_specs=out_specs, check_vma=False)
```

profile of v0, /device:TPU:0, one launch (start us, length us, event | category | flops | bytes accessed | tf_op | source)
XLA Modules:
  0.0 1997.7 jit_solution(15135687993326305070)
XLA Ops:
  22.3 20.6 %convolution_convert_fusion.1 = bf16[4,2048,1024]{2,1,0:T(8,128)(2,1)} fusion(bf16[261,1024]{1,0:T(8,128)(2,1)S(1)} %copy-done.60, f32[261]{0:T(512)S(1)} %copy-done.56, f32[4,2048]{1,0:T(4,128)S(1)} %add_rsqrt_fusion, f32[4,2048]{1,0:T(4,128)S(1)} %broadcast_multiply_fusion.2, bf16[4,2048,261]{1,0,2:T(4,128)(2,1)S(1)} %copy-done.3), kind=kOutput, calls=%fused_computation.4 | convolution fusion | flops 4397932544 | bytes 21654548 | tf_op jit(solution)/shard_map/ipc,cd->ipd/dot_general | solution.py:113
  42.9 20.6 %convolution_convert_fusion.2 = bf16[4,2048,1024]{2,1,0:T(8,128)(2,1)} fusion(bf16[261,1024]{1,0:T(8,128)(2,1)S(1)} %copy-done.58, f32[261]{0:T(512)S(1)} %copy-done.56, f32[4,2048]{1,0:T(4,128)S(1)} %add_rsqrt_fusion, f32[4,2048]{1,0:T(4,128)S(1)} %broadcast_multiply_fusion.2, bf16[4,2048,261]{1,0,2:T(4,128)(2,1)S(1)} %copy-done.3), kind=kOutput, calls=%fused_computation.5 | convolution fusion | flops 4397932544 | bytes 21654548 | tf_op jit(solution)/shard_map/ipc,cd->ipd/dot_general | solution.py:110
  67.2 18.3 fusion
  85.5 18.5 convolution_convert_fusion.5
  104.1 32.6 %psum.64 = bf16[4,512]{1,0:T(4,128)(2,1)S(1)} all-reduce(bf16[4,512]{1,0:T(4,128)(2,1)S(1)} %get-tuple-element.116), channel_id=1, replica_groups=mesh['item'=2,'lat'=4,'pix'=4] {'lat','pix'}, use_global_device_ids=true, to_apply=%region_6.7 | all-reduce | flops 2048 | bytes 8192 | tf_op jit(solution)/shard_map/psum | solution.py:128
  136.8 78.6 %all-reduce.5.cloned.1.call-done = bf16[4,512,1024]{2,1,0:T(8,128)(2,1)} async-done(((bf16[4,512,1024]{2,1,0:T(8,128)(2,1)}), bf16[4,512,1024]{2,1,0:T(8,128)(2,1)}) %all-reduce.5.cloned.1.call-update) | async-done | bytes 4194320 | tf_op jit(solution)/shard_map/psum | solution.py:127
  230.0 70.6 %all-gather.7.cloned.1.call-done = bf16[4,512,2048]{2,0,1:T(4,128)(2,1)} async-done(((bf16[4,32,2048]{2,0,1:T(4,128)(2,1)}), bf16[4,512,2048]{2,0,1:T(4,128)(2,1)}) %all-gather.7.cloned.1.call-update) | async-done | bytes 8388624 | tf_op jit(solution)/shard_map/all_gather | solution.py:144
  372.4 99.0 %reduce-scatter.11.cloned.1.call-done = bf16[4,32,2048]{2,1,0:T(8,128)(2,1)} async-done(((bf16[4,512,2048]{2,1,0:T(8,128)(2,1)}), bf16[4,32,2048]{2,1,0:T(8,128)(2,1)}) %reduce-scatter.11.cloned.1.call-update) | async-done | bytes 524304 | tf_op jit(solution)/shard_map/reduce_scatter | solution.py:198
  483.6 31.3 %all-gather = bf16[16,32,4]{1,2,0:T(4,128)(2,1)S(1)} all-gather(bf16[1,32,4]{1,2,0:T(4,128)(2,1)S(1)} %fusion.74), channel_id=1, replica_groups=mesh['item'=2,'lat'=4,'pix'=4] {'lat','pix'}, dimensions={0}, use_global_device_ids=true | all-gather | bytes 4352 | tf_op jit(solution)/shard_map/all_gather | solution.py:221
  515.0 19.0 all-gather.9.cloned.1.call-done
  533.9 16.2 multiply_convert_fusion.1
  633.4 16.3 convolution_bitcast_fusion.2
  663.9 19.6 fusion.25
  683.6 17.8 fusion.13
  714.3 40.6 %all-reduce = (f32[1024]{0:T(1024)}, f32[261]{0:T(512)}, f32[1024]{0:T(1024)}, f32[1024]{0:T(1024)}, f32[1024]{0:T(1024)}) all-reduce(f32[1024]{0:T(1024)S(1)} %get-tuple-element.99, f32[261]{0:T(512)S(1)} %get-tuple-element.90, f32[1024]{0:T(1024)S(1)} %get-tuple-element.97, ...), channel_id=1, replica_groups=mesh['item'=2,'lat'=4,'pix'=4] {'item','lat','pix'}, use_global_device_ids=true, to_apply=%region_39.40 | all-reduce | flops 4357 | bytes 34856 | tf_op jit(solution)/shard_map/psum | solution.py:291
  755.9 32.9 %reduce-scatter.27.cloned.1.call-done = f32[32,1024]{1,0:T(8,128)} async-done(((f32[1024,1024]{1,0:T(8,128)}), f32[32,1024]{1,0:T(8,128)}) %reduce-scatter.27.cloned.1.call-update) | async-done | bytes 131088 | tf_op jit(solution)/shard_map/reduce_scatter | solution.py:280
  788.8 149.3 %reduce-scatter.25.cloned.1.call-done = f32[32,1024]{1,0:T(8,128)} async-done(((f32[1024,1024]{1,0:T(8,128)}), f32[32,1024]{1,0:T(8,128)}) %reduce-scatter.25.cloned.1.call-update) | async-done | bytes 131088 | tf_op jit(solution)/shard_map/reduce_scatter | solution.py:279
  938.1 148.8 %reduce-scatter.29.cloned.1.call-done = f32[32,1024]{1,0:T(8,128)} async-done(((f32[1024,1024]{1,0:T(8,128)}), f32[32,1024]{1,0:T(8,128)}) %reduce-scatter.29.cloned.1.call-update) | async-done | bytes 131088 | tf_op jit(solution)/shard_map/reduce_scatter | solution.py:281
  1086.9 149.2 %reduce-scatter.21.cloned.1.call-done = f32[32,1024]{1,0:T(8,128)} async-done(((f32[1024,1024]{1,0:T(8,128)}), f32[32,1024]{1,0:T(8,128)}) %reduce-scatter.21.cloned.1.call-update) | async-done | bytes 131088 | tf_op jit(solution)/shard_map/reduce_scatter | solution.py:277
  1236.2 149.0 %reduce-scatter.19.cloned.1.call-done = f32[32,1024]{1,0:T(8,128)} async-done(((f32[1024,1024]{1,0:T(8,128)}), f32[32,1024]{1,0:T(8,128)}) %reduce-scatter.19.cloned.1.call-update) | async-done | bytes 131088 | tf_op jit(solution)/shard_map/reduce_scatter | solution.py:276
  1385.2 148.7 %reduce-scatter.17.cloned.1.call-done = f32[32,1024]{1,0:T(8,128)} async-done(((f32[1024,1024]{1,0:T(8,128)}), f32[32,1024]{1,0:T(8,128)}) %reduce-scatter.17.cloned.1.call-update) | async-done | bytes 131088 | tf_op jit(solution)/shard_map/reduce_scatter | solution.py:275
  1533.8 140.3 %all-reduce.7.cloned.1.call-done = (f32[261,1024]{1,0:T(8,128)}, f32[261,1024]{1,0:T(8,128)}) async-done(((f32[261,1024]{1,0:T(8,128)}, f32[261,1024]{1,0:T(8,128)}), (f32[261,1024]{1,0:T(8,128)}, f32[261,1024]{1,0:T(8,128)})) %all-reduce.7.cloned.1.call-update) | async-done | bytes 2138128 | tf_op jit(solution)/shard_map/psum | solution.py:291
  1674.1 162.2 %reduce-scatter.23.cloned.1.call-done = f32[32,3072]{1,0:T(8,128)} async-done(((f32[1024,3072]{1,0:T(8,128)}), f32[32,3072]{1,0:T(8,128)}) %reduce-scatter.23.cloned.1.call-update) | async-done | bytes 393232 | tf_op jit(solution)/shard_map/reduce_scatter | solution.py:278
  1836.3 149.8 %reduce-scatter.15.cloned.1.call-done = f32[32,1024]{1,0:T(8,128)} async-done(((f32[1024,1024]{1,0:T(8,128)}), f32[32,1024]{1,0:T(8,128)}) %reduce-scatter.15.cloned.1.call-update) | async-done | bytes 131088 | tf_op jit(solution)/shard_map/reduce_scatter | solution.py:274
  (261 shorter events, 232.4 us)
Async XLA Ops:
  7.2 326.6 %copy-start = (bf16[1024,1024]{1,0:T(8,128)(2,1)S(1)}, bf16[1024,1024]{1,0:T(8,128)(2,1)}, u32[]{:S(2)}) copy-start(bf16[1024,1024]{1,0:T(8,128)(2,1)} %param.35) | copy-start | bytes 6291460
  7.2 60.0 %all-gather.5.cloned.1.call-start = ((), (), s32[]{:S(2)}) async-start(), calls=%async_computation.10 | async-start | bytes 4456448 | tf_op jit(solution)/shard_map/all_gather | solution.py:107
  13.8 201.7 %all-reduce.5.cloned.1.call-start = ((), (), s32[]{:S(2)}) async-start(), calls=%async_computation.11 | async-start | bytes 8388608 | tf_op jit(solution)/shard_map/psum | solution.py:127
  19.8 23.1 %copy-start.39 = (f32[4,2048]{1,0:T(4,128)}, f32[4,2048]{1,0:T(4,128)S(1)}, u32[]{:S(2)}) copy-start(f32[4,2048]{1,0:T(4,128)S(1)} %broadcast_multiply_fusion.2) | copy-start | bytes 98308
  104.0 112.7 %copy-start.15 = (bf16[4,32,1024]{2,1,0:T(8,128)(2,1)S(1)}, bf16[4,32,1024]{2,1,0:T(8,128)(2,1)}, u32[]{:S(2)}) copy-start(bf16[4,32,1024]{2,1,0:T(8,128)(2,1)} %param.19) | copy-start | bytes 786436
  104.0 115.2 %copy-start.44 = (f32[1024]{0:T(1024)S(1)}, f32[1024]{0:T(1024)}, u32[]{:S(2)}) copy-start(f32[1024]{0:T(1024)} %param.28) | copy-start | bytes 12292
  104.1 196.6 %all-gather.7.cloned.1.call-start = ((), (), s32[]{:S(2)}) async-start(), calls=%async_computation.12 | async-start | bytes 8912896 | tf_op jit(solution)/shard_map/all_gather | solution.py:144
  226.7 244.7 %reduce-scatter.11.cloned.1.call-start = ((), (), s32[]{:S(2)}) async-start(), calls=%async_computation.13 | async-start | bytes 8912896 | tf_op jit(solution)/shard_map/reduce_scatter | solution.py:198
  368.3 165.6 %all-gather.9.cloned.1.call-start = ((), (), s32[]{:S(2)}) async-start(), calls=%async_computation.14 | async-start | bytes 4456448 | tf_op jit(solution)/shard_map/all_gather | solution.py:220
  372.4 99.0 %copy-start.35 = (bf16[16,8,8,128]{3,1,2,0:T(8,128)(2,1)}, bf16[16,8,8,128]{3,1,2,0:T(8,128)(2,1)S(1)}, u32[]{:S(2)}) copy-start(bf16[16,8,8,128]{3,1,2,0:T(8,128)(2,1)S(1)} %copy.148) | copy-start | bytes 786436
  480.7 103.3 %copy-start.7 = (f32[128,1024]{1,0:T(8,128)}, f32[128,1024]{1,0:T(8,128)S(1)}, u32[]{:S(2)}) copy-start(f32[128,1024]{1,0:T(8,128)S(1)} %multiply_add_fusion) | copy-start | bytes 1572868
  483.4 172.9 %reduce-scatter.13.cloned.1.call-start = ((), (), s32[]{:S(2)}) async-start(), calls=%async_computation.15 | async-start | bytes 4456448 | tf_op jit(solution)/shard_map/reduce_scatter | solution.py:235
  567.1 221.7 %reduce-scatter.27.cloned.1.call-start = ((), (), s32[]{:S(2)}) async-start(), calls=%async_computation.22 | async-start | bytes 4325376 | tf_op jit(solution)/shard_map/reduce_scatter | solution.py:280
  570.9 367.2 %reduce-scatter.25.cloned.1.call-start = ((), (), s32[]{:S(2)}) async-start(), calls=%async_computation.21 | async-start | bytes 4325376 | tf_op jit(solution)/shard_map/reduce_scatter | solution.py:279
  574.2 512.8 %reduce-scatter.29.cloned.1.call-start = ((), (), s32[]{:S(2)}) async-start(), calls=%async_computation.23 | async-start | bytes 4325376 | tf_op jit(solution)/shard_map/reduce_scatter | solution.py:281
  578.2 658.0 %reduce-scatter.21.cloned.1.call-start = ((), (), s32[]{:S(2)}) async-start(), calls=%async_computation.19 | async-start | bytes 4325376 | tf_op jit(solution)/shard_map/reduce_scatter | solution.py:277
  581.1 804.1 %reduce-scatter.19.cloned.1.call-start = ((), (), s32[]{:S(2)}) async-start(), calls=%async_computation.18 | async-start | bytes 4325376 | tf_op jit(solution)/shard_map/reduce_scatter | solution.py:276
  583.9 949.9 %reduce-scatter.17.cloned.1.call-start = ((), (), s32[]{:S(2)}) async-start(), calls=%async_computation.17 | async-start | bytes 4325376 | tf_op jit(solution)/shard_map/reduce_scatter | solution.py:275
  586.8 1087.4 %all-reduce.7.cloned.1.call-start = ((), (), s32[]{:S(2)}) async-start(), calls=%async_computation.24 | async-start | bytes 4325376 | tf_op jit(solution)/shard_map/psum | solution.py:291
  649.8 1186.5 %reduce-scatter.23.cloned.1.call-start = ((), (), s32[]{:S(2)}) async-start(), calls=%async_computation.20 | async-start | bytes 12976128 | tf_op jit(solution)/shard_map/reduce_scatter | solution.py:278
  656.3 1329.8 %reduce-scatter.15.cloned.1.call-start = ((), (), s32[]{:S(2)}) async-start(), calls=%async_computation.16 | async-start | bytes 4325376 | tf_op jit(solution)/shard_map/reduce_scatter | solution.py:274
  661.0 22.6 %slice-start = ((s8[4276224]{0:T(1024)(128)(4,1)}), s8[81920]{0:T(1024)(128)(4,1)S(1)}, s32[]{:S(2)}) async-start(s8[4276224]{0:T(1024)(128)(4,1)} %bitcast.147), calls=%async_computation.25 | async-start | bytes 163840
  707.9 47.0 %copy-start.8 = (f32[128,1024]{1,0:T(8,128)S(1)}, f32[128,1024]{1,0:T(8,128)}, u32[]{:S(2)}) copy-start(f32[128,1024]{1,0:T(8,128)} %copy-done.7) | copy-start | bytes 1572868
  713.3 1277.5 %copy-start.1 = (bf16[1024,1024]{1,0:T(8,128)(2,1)S(1)}, bf16[1024,1024]{1,0:T(8,128)(2,1)}, u32[]{:S(2)}) copy-start(bf16[1024,1024]{1,0:T(8,128)(2,1)} %param.35) | copy-start | bytes 6291460
  (58 other events, 389.3 us)
Sparse Core Ops, SparseCore 0:
  13.9 53.2 all-gather.4
  104.2 111.2 all-reduce.4
  226.8 73.7 all-gather.6
  368.4 102.9 reduce-scatter.10
  483.5 50.3 all-gather.8
  567.2 71.0 reduce-scatter.12
  641.1 147.6 reduce-scatter.26
  791.7 146.3 reduce-scatter.24
  940.9 145.9 reduce-scatter.28
  1089.6 146.5 reduce-scatter.20
  1239.0 146.0 reduce-scatter.18
  1387.9 145.9 reduce-scatter.16
  1540.2 133.9 all-reduce.6
  1681.6 154.6 reduce-scatter.22
  1839.0 147.0 reduce-scatter.14
where the time goes:
time: 2000 us
  waiting for transfers between devices  1500 us (75%)
  matrix products  282 us (14%)
  blocking collectives  105 us (5%)
  local copies, waits for them, and re-layouts  59.6 us (3%)
  other arithmetic  33.5 us (2%)
    reduce_scatter x1, waiting for transfers between devices, body(): lax.psum_scatter(self_in_grad, ('item', 'lat', 'pix'), scatter_dimension=...  162 us
    reduce_scatter x1, waiting for transfers between devices, body(): lax.psum_scatter(query_grad, ('item', 'lat', 'pix'), scatter_dimension=0,...  150 us
    reduce_scatter x1, waiting for transfers between devices, body(): lax.psum_scatter(self_out_grad, ('item', 'lat', 'pix'), scatter_dimension...  149 us
    reduce_scatter x1, waiting for transfers between devices, body(): lax.psum_scatter(first_down_grad, ('item', 'lat', 'pix'), scatter_dimensi...  149 us
    reduce_scatter x1, waiting for transfers between devices, body(): lax.psum_scatter(first_up_grad, ('item', 'lat', 'pix'), scatter_dimension...  149 us
    reduce_scatter x1, waiting for transfers between devices, body(): lax.psum_scatter(second_down_grad, ('item', 'lat', 'pix'), scatter_dimens...  149 us
    reduce_scatter x1, waiting for transfers between devices, body(): lax.psum_scatter(cross_out_grad, ('item', 'lat', 'pix'), scatter_dimensio...  149 us
    psum x1, waiting for transfers between devices, body(): lax.psum((key_grad, value_grad, cross_gain_grad, pixel_gain_grad, first_g...  140 us
  transfers between devices with their start and end apart: 15, of which 14 were waited for; matrix products, arithmetic and copies ran while one was open for 10% of the time, Pallas kernels for 0%

commit v1 on v0

v1 whole, which is shorter than its diff:
```python
import math

import jax
import jax.numpy as jnp
from jax import lax
from jax.experimental import pallas as pl
from jax.experimental.pallas import tpu as pltpu
from jax.sharding import PartitionSpec as P

HEADS = 8
EPS = 1e-05
LOG2E = 1.4426950408889634
LN2 = 0.6931471805599453
BF = jnp.bfloat16
F32 = jnp.float32
VM = pl.BlockSpec(memory_space=pltpu.VMEM)
SM = pl.BlockSpec(memory_space=pltpu.SMEM)
LIMIT = 58 * 1024 * 1024


def nn(a, b):
    return lax.dot_general(a, b, (((1,), (0,)), ((), ())), preferred_element_type=F32)


def nt(a, b):
    return lax.dot_general(a, b, (((1,), (1,)), ((), ())), preferred_element_type=F32)


def tn(a, b):
    return lax.dot_general(a, b, (((0,), (0,)), ((), ())), preferred_element_type=F32)


def stats(v):
    c = v - jnp.mean(v, axis=-1, keepdims=True)
    r = lax.rsqrt(jnp.mean(c * c, axis=-1, keepdims=True) + EPS)
    return c * r, r


def norm_back(scaled, n, r):
    return r * (
        scaled
        - jnp.mean(scaled, axis=-1, keepdims=True)
        - n * jnp.mean(scaled * n, axis=-1, keepdims=True)
    )


K0 = math.sqrt(2.0 / math.pi)
K1 = 0.044715


def gelu(v):
    return 0.5 * v * (1.0 + jnp.tanh(K0 * (v + K1 * v * v * v)))


def gelu_grad(v):
    t = jnp.tanh(K0 * (v + K1 * v * v * v))
    return 0.5 * (1.0 + t) + 0.5 * v * (1.0 - t * t) * (K0 * (1.0 + 3.0 * K1 * v * v))


def cost(flops, nbytes=0):
    return pl.CostEstimate(flops=int(flops), bytes_accessed=int(nbytes), transcendentals=0)


def call(kernel, outs, ins, scratch=(), flops=0, **kw):
    return pl.pallas_call(
        kernel,
        out_shape=tuple(jax.ShapeDtypeStruct(s, d) for s, d in outs),
        in_specs=[SM if a.dtype == jnp.int32 else VM for a in ins],
        out_specs=tuple(VM for _ in outs),
        scratch_shapes=list(scratch),
        compiler_params=pltpu.CompilerParams(vmem_limit_bytes=LIMIT),
        cost_estimate=cost(flops, 4000000),
        **kw,
    )(*ins)


def query_kernel(lat, gain, wq, wk, gcol, out, scr, *, scale):
    chans = wk.shape[0]
    n, _ = stats(lat[...].astype(F32))
    rounded = (n * gain[...]).astype(BF)
    query = nn(rounded, wq[...]).astype(BF)
    t = nt(wk[...], query) * gcol[...]
    t = (t - jnp.sum(t, axis=0, keepdims=True) / chans) * (scale * LOG2E)
    scr[...] = jnp.zeros(scr.shape, F32)
    scr[0:chans, :] = t
    out[...] = scr[...].astype(BF)


def pixel_norm_kernel(cnt, pix, out, eye, *, chans, tile):
    i, t = pl.program_id(0), pl.program_id(1)
    feat = out.shape[1]

    @pl.when((i == 0) & (t == 0))
    def _():
        rows = lax.broadcasted_iota(jnp.int32, eye.shape, 0)
        cols = lax.broadcasted_iota(jnp.int32, eye.shape, 1)
        eye[...] = (rows == cols).astype(F32).astype(BF)

    xt = nt(eye[...], pix[0])
    base = feat - 16
    mean = jnp.sum(xt, axis=0, keepdims=True) / chans
    low = xt[0:base] - mean
    row = lax.broadcasted_iota(jnp.int32, (16, tile), 0) + base
    high = jnp.where(row < chans, xt[base:feat] - mean, 0.0)
    var = (
        jnp.sum(low * low, axis=0, keepdims=True) + jnp.sum(high * high, axis=0, keepdims=True)
    ) / chans
    lane = lax.broadcasted_iota(jnp.int32, (1, tile), 1) + t * tile
    valid = jnp.where(lane < cnt[i], 1.0, 0.0)
    inv = lax.rsqrt(var + EPS) * valid
    inv_high = inv.astype(BF).astype(F32)
    out[0, 0:base, :] = (low * inv).astype(BF)
    high = high * inv
    high = jnp.where(row == chans, valid, high)
    high = jnp.where(row == chans + 1, valid, high)
    high = jnp.where(row == chans + 2, inv_high, high)
    high = jnp.where(row == chans + 3, inv - inv_high, high)
    out[0, base:feat, :] = high.astype(BF)


def cross_kernel(*refs, images, lat_rows, scale):
    pos = refs[0]
    pieces = refs[1:17]
    nt_ref = refs[17]
    p_out, qkt_out, mine, send = refs[18:22]
    qkt, qk, acc = refs[22:25]
    i, t = pl.program_id(0), pl.program_id(1)
    lpos, core, z = pos[0], pos[1], pos[2]
    group = 4 * lat_rows

    @pl.when((i == 0) & (t == 0))
    def _():
        for rl in range(4):
            for im in range(images):
                parts = [
                    pieces[rl * 4 + rz][:, lat_rows * im : lat_rows * (im + 1)].astype(F32)
                    for rz in range(4)
                ]
                v = pltpu.roll(jnp.concatenate(parts, axis=1), lat_rows * z, 1)
                at = pl.multiple_of(group * (lpos ^ rl), group)
                qkt[im, :, pl.ds(at, group)] = v.astype(BF)

    @pl.when(t == 0)
    def _():
        qk[...] = jnp.transpose(qkt[i].astype(F32), (1, 0)).astype(BF)
        qkt_out[0] = qkt[i]

    n = nt_ref[0]
    p = jnp.exp2(nn(qk[...], n)).astype(BF)
    p_out[0] = p
    part = nt(n, p)

    @pl.when(t == 0)
    def _():
        acc[...] = part

    @pl.when(t != 0)
    def _():
        acc[...] = acc[...] + part

    @pl.when(t == pl.num_programs(1) - 1)
    def _():
        split_halves(acc, mine, send, core, group)


def split_halves(acc, mine, send, core, group):
    for y in range(2):
        a = pl.multiple_of(2 * group * y + group * core, group)
        b = pl.multiple_of(2 * group * y + group * (1 - core), group)
        mine[0, :, group * y : group * (y + 1)] = acc[:, pl.ds(a, group)].astype(BF)
        send[0, :, group * y : group * (y + 1)] = acc[:, pl.ds(b, group)].astype(BF)


def pixel_back_kernel(*refs, chans, images):
    pos = refs[0]
    pieces = refs[1:9]
    nt_ref, p_ref, qkt_ref = refs[9:12]
    grad, mine, send = refs[12:15]
    gvt, gv, qktb, acc = refs[15:19]
    i, t = pl.program_id(0), pl.program_id(1)
    core, z = pos[1], pos[2]
    feat, lats = gv.shape[1], gv.shape[0]
    group = lats // 4
    base = feat - 16

    @pl.when((i == 0) & (t == 0))
    def _():
        for other in range(2):
            for rz in range(4):
                im = lax.rem(z + rz, 4)
                for y in range(2):
                    at = pl.multiple_of(2 * group * y + group * (core ^ other), group)
                    gvt[im, :, pl.ds(at, group)] = pieces[other * 4 + rz][
                        :, group * y : group * (y + 1)
                    ]

    @pl.when(t == 0)
    def _():
        gv[...] = jnp.transpose(gvt[i].astype(F32), (1, 0)).astype(BF)
        qktb[...] = (qkt_ref[0].astype(F32) * LN2).astype(BF)

    n = nt_ref[0]
    p = p_ref[0]
    ds = (p.astype(F32) * nn(gv[...], n)).astype(BF)
    part = nt(n, ds)
    dn = nn(qktb[...], ds) + nn(gvt[i], p)
    nf = n.astype(F32)
    low, high = nf[0:base], nf[base:feat]
    row = lax.broadcasted_iota(jnp.int32, high.shape, 0) + base
    inv = jnp.sum(
        jnp.where((row == chans + 2) | (row == chans + 3), high, 0.0), axis=0, keepdims=True
    )
    high = jnp.where(row < chans, high, 0.0)
    m2 = (
        jnp.sum(dn[0:base] * low, axis=0, keepdims=True)
        + jnp.sum(dn[base:feat] * high, axis=0, keepdims=True)
    ) / chans
    out = jnp.concatenate([inv * (dn[0:base] - low * m2), inv * (dn[base:feat] - high * m2)], axis=0)
    grad[0] = jnp.transpose(out, (1, 0))[:, 0:chans].astype(BF)

    @pl.when(t == 0)
    def _():
        acc[...] = part

    @pl.when(t != 0)
    def _():
        acc[...] = acc[...] + part

    @pl.when(t == pl.num_programs(1) - 1)
    def _():
        split_halves(acc, mine, send, core, group)


def first_kernel(pos, a_mine, a_recv, lat_mine, lat_recv, gcol, wv, co, g1, fu, fd, gs, si,
                 att_out, tot_out, res1_out, nt2_out, hid1_out, act1_out, res2_out, nt3_out, q_out, kv_out, lat):
    y = pos[3]
    half = lat_mine.shape[0]
    width = lat.shape[1]
    chans = wv.shape[0]
    lat[pl.ds(pl.multiple_of(half * y, half), half), :] = lat_mine[...]
    lat[pl.ds(pl.multiple_of(half * (1 - y), half), half), :] = lat_recv[...]
    a = a_mine[...].astype(F32) + a_recv[...].astype(F32)
    tot = a[chans : chans + 1, :]
    att = a[0:chans, :] / tot
    att_out[...] = att
    tot_out[...] = tot
    mixed = tn((att * gcol[...]).astype(BF), wv[...]).astype(BF)
    res1 = lat[...].astype(F32) + nn(mixed, co[...])
    res1_out[...] = res1
    n2, _ = stats(res1)
    nt2 = (n2 * g1[...]).astype(BF)
    nt2_out[...] = nt2
    hid = nn(nt2, fu[...])
    hid1_out[...] = hid
    act = gelu(hid).astype(BF)
    act1_out[...] = act
    res2 = res1 + nn(act, fd[...])
    res2_out[...] = res2
    n3, _ = stats(res2)
    nt3 = (n3 * gs[...]).astype(BF)
    nt3_out[...] = nt3
    kv_out[...] = nn(nt3, si[:, width : 3 * width]).astype(BF)
    q_out[...] = nn(nt3, si[:, 0:width]).astype(BF)


def second_kernel(pos, q, kv, kv2, res2, cot_mine, cot_recv, so, g2, su, sd,
                  out, selfr_out, sent3_out, back3_out, nt4_out, act2_out, hg2_out, gain_out, dq_out, dkv_out, dkv2_out,
                  prob, cot, mixed_scr, tots):
    y = pos[3]
    half = cot_mine.shape[0]
    rows, width = res2.shape
    hd = width // HEADS
    hs = 1.0 / math.sqrt(hd)
    cot[pl.ds(pl.multiple_of(half * y, half), half), :] = cot_mine[...]
    cot[pl.ds(pl.multiple_of(half * (1 - y), half), half), :] = cot_recv[...]
    for h in range(HEADS):
        cols = slice(h * hd, (h + 1) * hd)
        vcols = slice(width + h * hd, width + (h + 1) * hd)
        qh = q[:, cols]
        pa = jnp.exp2(nt(qh, kv[:, cols]) * (hs * LOG2E))
        pb = jnp.exp2(nt(qh, kv2[:, cols]) * (hs * LOG2E))
        tot = jnp.sum(pa, axis=1, keepdims=True) + jnp.sum(pb, axis=1, keepdims=True)
        pa, pb = pa.astype(BF), pb.astype(BF)
        prob[h, :, 0:rows] = pa
        prob[h, :, rows : 2 * rows] = pb
        rt = 1.0 / tot
        tots[h] = rt
        mixed_scr[:, cols] = (nn(pa, kv[:, vcols]) + nn(pb, kv2[:, vcols])) * rt
    selfr = mixed_scr[...].astype(BF)
    selfr_out[...] = selfr
    res3 = res2[...] + nn(selfr, so[...])
    n4, r4 = stats(res3)
    nt4 = (n4 * g2[...]).astype(BF)
    nt4_out[...] = nt4
    hid = nn(nt4, su[...])
    act = gelu(hid).astype(BF)
    act2_out[...] = act
    out[...] = (res3 + nn(act, sd[...])).astype(BF)
    hg = (nt(cot[...], sd[...]) * gelu_grad(hid)).astype(BF)
    hg2_out[...] = hg
    ng = nt(hg, su[...])
    gain_out[...] = jnp.sum(ng * n4, axis=0, keepdims=True)
    back3 = cot[...].astype(F32) + norm_back(ng * g2[...], n4, r4)
    back3_out[...] = back3
    sent3 = back3.astype(BF)
    sent3_out[...] = sent3
    mg_all = nt(sent3, so[...]).astype(BF)
    for h in range(HEADS):
        cols = slice(h * hd, (h + 1) * hd)
        vcols = slice(width + h * hd, width + (h + 1) * hd)
        mg = mg_all[:, cols].astype(F32)
        rt = tots[h]
        ng_h = (mg * rt).astype(BF)
        tg = -jnp.sum(mg * mixed_scr[:, cols], axis=1, keepdims=True) * rt
        qh = q[:, cols]
        dq = None
        for src, dst, at in ((kv, dkv_out, 0), (kv2, dkv2_out, rows)):
            p = prob[h, :, at : at + rows]
            sg = (p.astype(F32) * (nt(ng_h, src[:, vcols]) + tg)).astype(BF)
            d = nn(sg, src[:, cols])
            dq = d if dq is None else dq + d
            dst[:, cols] = (tn(sg, qh) * hs).astype(dst.dtype)
            dst[:, vcols] = tn(p, ng_h).astype(dst.dtype)
        dq_out[:, cols] = (dq * hs).astype(BF)


def third_kernel(dq, dkv, dkv2, back3, res2, res1, hid1, att, tot, gcol, wv, co, g1, fu, fd, gs, si, gain2,
                 pg_out, sent2_out, hg1_out, back1_out, gv_out, ht_out, scr):
    rows, width = back3.shape
    chans = wv.shape[0]
    feat = scr.shape[0]
    base = feat - 16
    pg_out[:, 0:width] = dq[...]
    pg_out[:, width : 3 * width] = (dkv[...] + dkv2[...].astype(F32)).astype(BF)
    ng = nt(pg_out[...], si[...])
    n3, r3 = stats(res2[...])
    gain_self = jnp.sum(ng * n3, axis=0, keepdims=True)
    back2 = back3[...] + norm_back(ng * gs[...], n3, r3)
    sent2 = back2.astype(BF)
    sent2_out[...] = sent2
    hg = (nt(sent2, fd[...]) * gelu_grad(hid1[...])).astype(BF)
    hg1_out[...] = hg
    ng = nt(hg, fu[...])
    n2, r2 = stats(res1[...])
    gain_first = jnp.sum(ng * n2, axis=0, keepdims=True)
    back1 = back2 + norm_back(ng * g1[...], n2, r2)
    back1_out[...] = back1
    sent1 = back1.astype(BF)
    ag = nt(sent1, co[...]).astype(BF)
    rt = 1.0 / tot[...]
    raw = nt(wv[...], ag) * (rt * gcol[...])
    tg = -jnp.sum(att[...] * raw, axis=0, keepdims=True)
    raw = raw - jnp.sum(raw, axis=0, keepdims=True) / chans
    scr[...] = jnp.zeros(scr.shape, F32)
    scr[0:chans, :] = raw
    gv_out[0:base, :] = scr[0:base, :].astype(BF)
    row = lax.broadcasted_iota(jnp.int32, (16, rows), 0) + base
    tg_high = tg.astype(BF).astype(F32)
    high = jnp.where(row == chans, tg_high, scr[base:feat, :])
    high = jnp.where(row == chans + 1, tg - tg_high, high)
    gv_out[base:feat, :] = high.astype(BF)
    scr[0:chans, :] = att[...]
    ht = nn(scr[...].astype(BF), sent1)
    ht_out[0:base, :] = (0.5 * ht[0:base]).astype(BF)
    row = lax.broadcasted_iota(jnp.int32, (16, width), 0) + base
    high = ht[base:feat]
    for k, v in enumerate((gain_first, gain_self, gain2[...])):
        v_high = v.astype(BF).astype(F32)
        high = jnp.where(row == chans + 2 * k, v_high, high)
        high = jnp.where(row == chans + 2 * k + 1, v - v_high, high)
    ht_out[base:feat, :] = (0.5 * high).astype(BF)


def last_kernel(b_mine, b_recv, lat, back1, gain, gcol, wq, wk, out, gt_out, scr, *, scale):
    chans, width = wk.shape
    feat = scr.shape[0]
    base = feat - 16
    b = (b_mine[...].astype(F32) + b_recv[...].astype(F32)) * (scale * LN2 * LOG2E)
    bs = b[0:chans, :]
    rows_grad = tn((bs * gcol[...]).astype(BF), wk[...]).astype(BF)
    ng = nt(rows_grad, wq[...])
    n, r = stats(lat[...].astype(F32))
    rounded = (n * gain[...]).astype(BF)
    gain_grad = jnp.sum(ng * n, axis=0, keepdims=True)
    out[...] = (back1[...] + norm_back(ng * gain[...], n, r)).astype(BF)
    scr[...] = jnp.zeros(scr.shape, F32)
    scr[0:chans, :] = bs
    gt = nn(scr[...].astype(BF), rounded)
    gt_out[0:base, :] = gt[0:base].astype(BF)
    row = lax.broadcasted_iota(jnp.int32, (16, width), 0) + base
    high = gt[base:feat]
    g_high = gain_grad.astype(BF).astype(F32)
    high = jnp.where(row == chans, g_high, high)
    high = jnp.where(row == chans + 1, gain_grad - g_high, high)
    gt_out[base:feat, :] = high.astype(BF)


def value_kernel(pos, ht, gcol, wv, co, value_out, cross_out, vsum_out, gains_out):
    chans, width = wv.shape
    rows = cross_out.shape[0]
    h = ht[...].astype(F32)
    hb = ht[0:chans, :]
    v = nt(hb, co[...])
    vsum_out[...] = jnp.sum(v * wv[...].astype(F32), axis=1, keepdims=True)
    value_out[...] = v * gcol[...]
    one = own_columns(width, rows, pos[4])
    wsel = (nn(wv[...], one) * gcol[...]).astype(BF)
    cross_out[...] = tn(wsel, hb)
    for k in range(3):
        gains_out[k : k + 1, :] = (
            h[chans + 2 * k : chans + 2 * k + 1, :] + h[chans + 2 * k + 1 : chans + 2 * k + 2, :]
        )


def own_columns(width, rows, index):
    r = lax.broadcasted_iota(jnp.int32, (width, rows), 0)
    c = lax.broadcasted_iota(jnp.int32, (width, rows), 1)
    return (r == c + index * rows).astype(F32).astype(BF)


def key_kernel(pos, gt, gcol, wk, wq, vsum, key_out, query_out, psum_out, gain_out):
    chans, width = wk.shape
    rows = query_out.shape[0]
    g = gt[...].astype(F32)
    gb = gt[0:chans, :]
    k = nn(gb, wq[...])
    psum_out[...] = jnp.sum(k * wk[...].astype(F32), axis=1, keepdims=True) + vsum[...]
    key_out[...] = k * gcol[...]
    one = own_columns(width, rows, pos[4])
    sel = (nn(gb, one) * gcol[...]).astype(BF)
    query_out[...] = tn(sel, wk[...])
    gain_out[...] = g[chans : chans + 1, :] + g[chans + 1 : chans + 2, :]


def swap(x, kind, lat):
    if kind == "core":
        perm = [(s, s ^ 1) for s in range(lat)]
    else:
        perm = [(s, s ^ 2) for s in range(lat)]
    return lax.ppermute(x, "lat", perm)


def around(x, n):
    got = [x]
    for r in range(1, n):
        got.append(lax.ppermute(x, "pix", [((d + r) % n, d) for d in range(n)]))
    return got


def sum_over(x):
    return jnp.sum(x.astype(F32), axis=0)


def all_sum(x, items, lat):
    feat, width = x.shape
    parts = items * lat
    lanes = width // parts
    x = jnp.transpose(x.reshape(feat, parts, lanes), (1, 0, 2))
    x = lax.all_to_all(x, ("item", "lat"), 0, 0, tiled=True)
    x = sum_over(x).astype(BF)
    x = sum_over(lax.all_gather(x, "pix", axis=0)).astype(BF)
    x = lax.all_gather(x, ("item", "lat"), axis=0)
    return jnp.transpose(x, (1, 0, 2)).reshape(feat, width)


def reduce_units(units, items, lat, pix, yy, core):
    width = units[0][0].shape[1]
    chunk = width // (2 * items)
    outs = []
    for left, right in units:
        rows = left.shape[0]
        sel = lax.dynamic_index_in_dim(left.reshape(rows, items, 2, chunk), yy, 2, keepdims=False)
        outs.append(
            lax.dot_general(
                sel.reshape(rows, items * chunk),
                right,
                (((0,), (0,)), ((), ())),
                preferred_element_type=F32,
            ).astype(BF)
        )
    cols = [o.shape[1] for o in outs]
    x = jnp.concatenate(outs, axis=1) if len(outs) > 1 else outs[0]
    x = x.reshape(items, 2, chunk // 2, sum(cols))
    mine = lax.dynamic_index_in_dim(x, core, 1, keepdims=False)
    give = lax.dynamic_index_in_dim(x, 1 - core, 1, keepdims=False)
    got = swap(give, "core", lat)
    x = (mine.astype(F32) + got.astype(F32)).astype(BF)
    x = sum_over(lax.all_to_all(x, "item", 0, 0, tiled=True)).astype(BF)
    x = x.reshape(pix, chunk // (2 * pix), sum(cols))
    x = sum_over(lax.all_to_all(x, "pix", 0, 0, tiled=True))
    res, at = [], 0
    for c in cols:
        res.append(x[:, at : at + c])
        at += c
    return res


def body(
    latents,
    pixels,
    size_ids,
    cross_gain,
    pixel_gain,
    query_weight,
    key_weight,
    value_weight,
    cross_output,
    first_gain,
    first_up,
    first_down,
    self_gain,
    self_inputs,
    self_output,
    second_gain,
    second_up,
    second_down,
    cotangent,
):
    images, lat_rows, width = latents.shape
    pix_rows, chans = pixels.shape[1:]
    lat, pix, items = lax.axis_size("lat"), lax.axis_size("pix"), lax.axis_size("item")
    assert lat == 4 and pix == 4 and images == pix
    feat = -(-(chans + 4) // 16) * 16
    l, z, it = lax.axis_index("lat"), lax.axis_index("pix"), lax.axis_index("item")
    core, yy = l % 2, l // 2
    block = l * pix + z
    pos = jnp.stack([l, core, z, yy, it * (lat * pix) + block]).astype(jnp.int32)
    rows = images * lat_rows
    lats = lat * rows
    scale = 1.0 / math.sqrt(width)
    factor = jnp.where(size_ids == 0, 25, jnp.where(size_ids == 1, 49, 81)).astype(jnp.int32)
    counts = pix_rows * (lat * pix) * factor // 81 - block * pix_rows
    gcol = pixel_gain.reshape(chans, 1)
    row = lambda v: v.reshape(1, width)

    (qkt,) = call(
        lambda *r: query_kernel(*r, scale=scale),
        [((feat, rows), BF)],
        [latents.reshape(rows, width), row(cross_gain), query_weight, key_weight, gcol],
        [pltpu.VMEM((feat, rows), F32)],
        flops=2 * rows * width * width,
    )
    level = around(qkt, pix)
    level_y = [swap(v, "y", lat) for v in level]
    pieces = {0: level, 2: level_y}
    pieces[1] = [swap(v, "core", lat) for v in level]
    pieces[3] = [swap(v, "core", lat) for v in level_y]

    tile = min(1024, pix_rows)
    tiles = pix_rows // tile
    params = pltpu.CompilerParams(
        dimension_semantics=("arbitrary", "arbitrary"), vmem_limit_bytes=LIMIT
    )
    normed = pl.pallas_call(
        lambda *r: pixel_norm_kernel(*r, chans=chans, tile=tile),
        grid=(images, tiles),
        in_specs=[SM, pl.BlockSpec((1, tile, chans), lambda i, t: (i, t, 0))],
        out_specs=pl.BlockSpec((1, feat, tile), lambda i, t: (i, 0, t)),
        out_shape=jax.ShapeDtypeStruct((images, feat, pix_rows), BF),
        scratch_shapes=[pltpu.VMEM((feat, chans), BF)],
        compiler_params=params,
        cost_estimate=cost(images * pix_rows * 512 * feat * 4, images * pix_rows * feat * 4),
    )(counts, pixels)

    both = jnp.concatenate([latents, cotangent], axis=1)
    both = lax.all_to_all(both, "pix", 0, 0, tiled=True)
    lat_mine = both[:, :lat_rows].reshape(rows, width)
    cot_mine = both[:, lat_rows:].reshape(rows, width)
    lat_recv = swap(lat_mine, "y", lat)
    cot_recv = swap(cot_mine, "y", lat)

    whole = lambda a: pl.BlockSpec(a.shape, lambda i, t: (0,) * a.ndim)
    half_spec = pl.BlockSpec((1, feat, lats // 2), lambda i, t: (i, 0, 0))
    half_shape = jax.ShapeDtypeStruct((images, feat, lats // 2), BF)
    flat = [v for rl in range(4) for v in pieces[rl]]
    powered, qkt_all, mine, give = pl.pallas_call(
        lambda *r: cross_kernel(*r, images=images, lat_rows=lat_rows, scale=scale),
        grid=(images, tiles),
        in_specs=[SM]
        + [whole(v) for v in flat]
        + [pl.BlockSpec((1, feat, tile), lambda i, t: (i, 0, t))],
        out_specs=(
            pl.BlockSpec((1, lats, tile), lambda i, t: (i, 0, t)),
            pl.BlockSpec((1, feat, lats), lambda i, t: (i, 0, 0)),
            half_spec,
            half_spec,
        ),
        out_shape=(
            jax.ShapeDtypeStruct((images, lats, pix_rows), BF),
            jax.ShapeDtypeStruct((images, feat, lats), BF),
            half_shape,
            half_shape,
        ),
        scratch_shapes=[
            pltpu.VMEM((images, feat, lats), BF),
            pltpu.VMEM((lats, feat), BF),
            pltpu.VMEM((feat, lats), F32),
        ],
        compiler_params=params,
        cost_estimate=cost(images * pix_rows * 512 * lats * 4, images * pix_rows * lats * 3),
    )(pos, *flat, normed)

    def to_owner(mine, give):
        got = swap(give, "core", lat)
        x = (mine.astype(F32) + got.astype(F32)).astype(BF)
        return sum_over(lax.all_to_all(x, "pix", 0, 0, tiled=True))

    a_mine = to_owner(mine, give).astype(BF)
    a_recv = swap(a_mine, "y", lat)
    r2 = 2 * rows
    sq = (r2, width)
    att, tot, res1, nt2, hid1, act1, res2, nt3, q, kv = call(
        first_kernel,
        [((chans, r2), F32), ((1, r2), F32), (sq, F32), (sq, BF), (sq, F32), (sq, BF), (sq, F32), (sq, BF), (sq, BF), ((r2, 2 * width), BF)],
        [pos, a_mine, a_recv, lat_mine, lat_recv, gcol, value_weight, cross_output, row(first_gain), first_up, first_down, row(self_gain), self_inputs],
        [pltpu.VMEM(sq, BF)],
        flops=2 * r2 * width * width * 6,
    )
    kv2 = swap(kv, "core", lat)
    out, selfr, sent3, back3, nt4, act2, hg2, gain2, dq, dkv, dkv_send = call(
        second_kernel,
        [(sq, BF), (sq, BF), (sq, BF), (sq, F32), (sq, BF), (sq, BF), (sq, BF), ((1, width), F32), (sq, BF), ((r2, 2 * width), F32), ((r2, 2 * width), BF)],
        [pos, q, kv, kv2, res2, cot_mine, cot_recv, self_output, row(second_gain), second_up, second_down],
        [
            pltpu.VMEM((HEADS, r2, 2 * r2), BF),
            pltpu.VMEM(sq, BF),
            pltpu.VMEM(sq, F32),
            pltpu.VMEM((HEADS, r2, 1), F32),
        ],
        flops=2 * r2 * width * width * 10,
    )
    dkv2 = swap(dkv_send, "core", lat)
    pg, sent2, hg1, back1, gvt, ht = call(
        third_kernel,
        [((r2, 3 * width), BF), (sq, BF), (sq, BF), (sq, F32), ((feat, r2), BF), ((feat, width), BF)],
        [dq, dkv, dkv2, back3, res2, res1, hid1, att, tot, gcol, value_weight, cross_output, row(first_gain), first_up, first_down, row(self_gain), self_inputs, gain2],
        [pltpu.VMEM((feat, r2), F32)],
        flops=2 * r2 * width * width * 7,
    )
    gv_level = around(gvt, pix)
    gv_flat = gv_level + [swap(v, "core", lat) for v in gv_level]

    pixel_grad, mine, give = pl.pallas_call(
        lambda *r: pixel_back_kernel(*r, chans=chans, images=images),
        grid=(images, tiles),
        in_specs=[SM]
        + [whole(v) for v in gv_flat]
        + [
            pl.BlockSpec((1, feat, tile), lambda i, t: (i, 0, t)),
            pl.BlockSpec((1, lats, tile), lambda i, t: (i, 0, t)),
            pl.BlockSpec((1, feat, lats), lambda i, t: (i, 0, 0)),
        ],
        out_specs=(
            pl.BlockSpec((1, tile, chans), lambda i, t: (i, t, 0)),
            half_spec,
            half_spec,
        ),
        out_shape=(
            jax.ShapeDtypeStruct((images, pix_rows, chans), BF),
            half_shape,
            half_shape,
        ),
        scratch_shapes=[
            pltpu.VMEM((images, feat, lats), BF),
            pltpu.VMEM((lats, feat), BF),
            pltpu.VMEM((feat, lats), BF),
            pltpu.VMEM((feat, lats), F32),
        ],
        compiler_params=params,
        cost_estimate=cost(images * pix_rows * 512 * lats * 8, images * pix_rows * lats * 3),
    )(pos, *gv_flat, normed, powered, qkt_all)

    own = to_owner(mine, give).astype(BF)
    b_mine = lax.dynamic_slice_in_dim(own, yy * rows, rows, 1)
    b_recv = swap(lax.dynamic_slice_in_dim(own, (1 - yy) * rows, rows, 1), "y", lat)
    back1_own = lax.dynamic_slice_in_dim(back1, yy * rows, rows, 0)
    latent_grad, gt = call(
        lambda *r: last_kernel(*r, scale=scale),
        [((rows, width), BF), ((feat, width), BF)],
        [b_mine, b_recv, lat_mine, back1_own, row(cross_gain), gcol, query_weight, key_weight],
        [pltpu.VMEM((feat, rows), F32)],
        flops=2 * rows * width * width * 2,
    )

    def back_home(x):
        x = x.reshape(pix, lat_rows, width)
        return lax.all_to_all(x, "pix", 0, 0, tiled=True)

    latents_out = back_home(lax.dynamic_slice_in_dim(out, yy * rows, rows, 0))
    latent_grad = back_home(latent_grad)

    own_rows = width // (items * lat * pix)
    ht = all_sum(ht, items, lat)
    value_grad, cross_out_grad, vsum, gains = call(
        value_kernel,
        [((chans, width), F32), ((own_rows, width), F32), ((chans, 1), F32), ((3, width), F32)],
        [pos, ht, gcol, value_weight, cross_output],
        flops=2 * chans * width * width,
    )
    second_up_grad, second_down_grad, self_out_grad = reduce_units(
        [(nt4, hg2), (act2, cot_rows(cot_mine, cot_recv, yy)), (selfr, sent3)],
        items, lat, pix, yy, core,
    )
    (self_in_grad,) = reduce_units([(nt3, pg)], items, lat, pix, yy, core)
    first_up_grad, first_down_grad = reduce_units(
        [(nt2, hg1), (act1, sent2)], items, lat, pix, yy, core
    )
    gt = all_sum(gt, items, lat)
    key_grad, query_grad, psum, cross_gain_grad = call(
        key_kernel,
        [((chans, width), F32), ((own_rows, width), F32), ((chans, 1), F32), ((1, width), F32)],
        [pos, gt, gcol, key_weight, query_weight, vsum],
        flops=2 * chans * width * width,
    )
    return (
        latents_out,
        latent_grad,
        pixel_grad,
        query_grad,
        cross_out_grad,
        first_up_grad,
        first_down_grad,
        self_in_grad,
        self_out_grad,
        second_up_grad,
        second_down_grad,
        key_grad,
        value_grad,
        cross_gain_grad.reshape(width),
        psum.reshape(chans),
        gains[0],
        gains[1],
        gains[2],
    )


def cot_rows(mine, recv, yy):
    first = jnp.where(yy == 0, mine, recv)
    second = jnp.where(yy == 0, recv, mine)
    return jnp.concatenate([first, second], axis=0)


def solution(mesh):
    split = P("item", ("lat", "pix"), None)
    in_specs = (split, split, P("item")) + (P(),) * 15 + (split,)
    grads = P(("item", "lat", "pix"), None)
    out_specs = (split, split, split) + (grads,) * 8 + (P(),) * 7
    return jax.shard_map(body, mesh=mesh, in_specs=in_specs, out_specs=out_specs, check_vma=False)
```

time: 2000 us -> 465 us (0.23)
  waiting for transfers between devices: 1500 us -> 120 us
  matrix products: 282 us -> 5.27 us
  Pallas kernels: 0 us -> 103 us
  starting transfers between devices: 1.31 us -> 77.9 us
  blocking collectives: 105 us -> 60.8 us
    reduce_scatter x10 -> x0, waiting for transfers between devices: 1190 us -> none  [the longest x1 162 us: body(): lax.psum_scatter(self_in_grad, ('item', 'lat', 'pix'), scatter_dimension=...]
    dot_general x42 -> x6, matrix products: 282 us -> 5.27 us  [reduce_units(): lax.dot_general(sel.reshape(rows, items * chunk), right, (((0,), (0,)), (...]
    psum x2 -> x0, waiting for transfers between devices: 219 us -> none  [the longest x1 140 us: body(): lax.psum((key_grad, value_grad, cross_gain_grad, pixel_gain_grad, first_g...]
    pallas_call x0 -> x10, Pallas kernels: none -> 103 us  [the longest x7 56.9 us: call(): pl.pallas_call(kernel, out_shape=tuple((jax.ShapeDtypeStruct(s, d) for s,...]
    all_to_all x0 -> x13, waiting for transfers between devices: none -> 98.4 us  [the longest x3 33.6 us: reduce_units(): x = sum_over(lax.all_to_all(x, 'item', 0, 0, tiled=True)).astype(BF)]
    all_gather x3 -> x0, waiting for transfers between devices: 93.3 us -> none  [the longest x1 70.6 us: body(): lax.all_gather(projected[:, :, width:], ('lat', 'pix'), axis=1, tiled=True)]
    psum x2 -> x0, blocking collectives: 73.2 us -> none  [the longest x1 40.6 us: body(): lax.psum((key_grad, value_grad, cross_gain_grad, pixel_gain_grad, first_g...]
    all_to_all x0 -> x13, starting transfers between devices: none -> 51.6 us  [the longest x3 12.7 us: reduce_units(): x = sum_over(lax.all_to_all(x, 'item', 0, 0, tiled=True)).astype(BF)]
  transfers between devices with their start and end apart: 15 -> 46, of which waited for: 14 -> 17; matrix products, arithmetic and copies ran while one was open for 10% -> 17% of each run, Pallas kernels for 0% -> 12%
where the time goes in v1:
time: 465 us; the launch traced here: 457 us
  waiting for transfers between devices  120 us (26%)
  Pallas kernels  103 us (22%)
  starting transfers between devices  77.9 us (17%)
  blocking collectives  60.8 us (13%)
  local copies, waits for them, and re-layouts  60.6 us (13%)
  other arithmetic  27.9 us (6%)
  matrix products  5.27 us (1%)
    pallas_call x7, Pallas kernels, call(): pl.pallas_call(kernel, out_shape=tuple((jax.ShapeDtypeStruct(s, d) for s,...  56.9 us
    all_gather x2, blocking collectives, all_sum(): x = sum_over(lax.all_gather(x, 'pix', axis=0)).astype(BF)  41.7 us
    unnamed x102, local copies, waits for them, and re-layouts  34.2 us
    all_to_all x3, waiting for transfers between devices, reduce_units(): x = sum_over(lax.all_to_all(x, 'item', 0, 0, tiled=True)).astype(BF)  33.6 us
    all_to_all x2, waiting for transfers between devices, to_owner(): return sum_over(lax.all_to_all(x, 'pix', 0, 0, tiled=True))  22.9 us
    pallas_call x1, Pallas kernels, body(): pl.pallas_call(lambda *r: pixel_back_kernel(*r, chans=chans, images=image...  21.3 us
    all_gather x2, blocking collectives, all_sum(): x = lax.all_gather(x, ('item', 'lat'), axis=0)  19.1 us
    pallas_call x1, Pallas kernels, body(): pl.pallas_call(lambda *r: cross_kernel(*r, images=images, lat_rows=lat_ro...  15.3 us
  transfers between devices with their start and end apart: 46, of which 17 were waited for; matrix products, arithmetic and copies ran while one was open for 17% of the time, Pallas kernels for 12%

profile of v1, /device:TPU:0, one launch (start us, length us, event | category | flops | bytes accessed | tf_op | source)
XLA Modules:
  0.0 457.3 jit_solution(3052919561917382745)
XLA Ops:
  5.5 5.1 %collective-permute-start = (bf16[272,128]{1,0:T(8,128)(2,1)}, bf16[272,128]{1,0:T(8,128)(2,1)S(1)}, u32[]{:S(2)}, u32[]{:S(2)}) collective-permute-start(bf16[272,128]{1,0:T(8,128)(2,1)} %shard_map.322.r_1_), channel_id=1, source_target_pairs={{1,0},{2,1},{3,2},{0,3},{5,4},{6,5},{7,6},{4,7},{9,8},{10,9},{11,1... | collective-permute-start | bytes 208904 | tf_op jit(solution)/shard_map/ppermute | solution.py:446
  20.4 10.4 %copy.74.r_1_ = bf16[4,2048,261]{2,1,0:T(8,128)(2,1)} copy(bf16[4,2048,261]{1,0,2:T(4,128)(2,1)} %param.20) | data formatting | bytes 8552448 | tf_op args[1]
  32.1 9.7 %shard_map.323.r_17_.r_9_ = bf16[4,272,2048]{2,1,0:T(8,128)(2,1)} custom-call(s32[4]{0:T(128)} %fusion.7.r_0_, bf16[4,2048,261]{2,1,0:T(8,128)(2,1)} %copy.74.r_1_), custom_call_target="tpu_custom_call" | custom-call | flops 4563402752 | bytes 8912896 | tf_op jit(solution)/shard_map/pallas_call | solution.py:554
  43.9 15.3 %shard_map.324 = (bf16[4,512,2048]{2,1,0:T(8,128)(2,1)}, bf16[4,272,512]{2,1,0:T(8,128)(2,1)}, bf16[4,272,256]{2,1,0:T(8,128)(2,1)}, bf16[4,272,256]{2,1,0:T(8,128)(2,1)}) custom-call(s32[5]{0:T(128)} %stack.23.r_0_.pos, bf16[272,128]{1,0:T(8,128)(2,1)} %shard_map.322.r_1_, bf16[272,128]{1,0:T(8,128)(2,1)} %copy-done.30, bf16[272,128]{1,0:T(8,128)(2,1)} %copy-done.31, ...), custom_call_target="tpu_custom_call" | custom-call | flops 8589934592 | bytes 12582912 | tf_op jit(solution)/shard_map/pallas_call | solution.py:576
  65.0 14.0 %all-to-all-done.1 = bf16[4,64,1024]{2,1,0:T(8,128)(2,1)S(1)} async-done(((bf16[4,64,1024]{2,1,0:T(8,128)(2,1)}), bf16[4,64,1024]{2,1,0:T(8,128)(2,1)S(1)}, u32[]{:S(2)}, u32[]{:S(2)}) %all-to-all-start.1) | async-done | bytes 524320 | tf_op jit(solution)/shard_map/all_to_all | solution.py:566
  84.4 13.2 %all-to-all-done = bf16[4,272,256]{2,1,0:T(8,128)(2,1)S(1)} async-done(((bf16[4,272,256]{2,1,0:T(8,128)(2,1)}), bf16[4,272,256]{2,1,0:T(8,128)(2,1)S(1)}, u32[]{:S(2)}, u32[]{:S(2)}) %all-to-all-start) | async-done | bytes 557088 | tf_op jit(solution)/shard_map/all_to_all | solution.py:606
  103.5 10.7 %shard_map.325 = (f32[261,256]{1,0:T(8,128)}, f32[1,256]{1,0:T(1,128)}, f32[256,1024]{1,0:T(8,128)}, bf16[256,1024]{1,0:T(8,128)(2,1)}, f32[256,1024]{1,0:T(8,12...) custom-call(s32[5]{0:T(128)} %stack.23.r_0_.pos, ...), custom_call_target="tpu_custom_call" | custom-call | flops 3221225472 | bytes 4000000 | tf_op jit(solution)/shard_map/pallas_call | solution.py:65
  115.9 7.1 %collective-permute-done.19.cot_recv = bf16[128,1024]{1,0:T(8,128)(2,1)S(1)} collective-permute-done((bf16[128,1024]{1,0:T(8,128)(2,1)S(1)}, bf16[128,1024]{1,0:T(8,128)(2,1)S(1)}, u32[]{:S(2)}, u32[]{:S(2)}) %collective-permute-start.19) | collective-permute-done | bytes 262176 | tf_op jit(solution)/shard_map/ppermute | solution.py:440
  129.2 16.7 %shard_map.326 = (bf16[256,1024]{1,0:T(8,128)(2,1)}, bf16[256,1024]{1,0:T(8,128)(2,1)}, bf16[256,1024]{1,0:T(8,128)(2,1)}, f32[256,1024]{1,0:T(8,128)}, bf16[256...) custom-call(s32[5]{0:T(128)} %stack.23.r_0_.pos, ...), custom_call_target="tpu_custom_call" | custom-call | flops 5368709120 | bytes 4000000 | tf_op jit(solution)/shard_map/pallas_call | solution.py:65
  165.3 13.5 %shard_map.327 = (bf16[256,3072]{1,0:T(8,128)(2,1)}, bf16[256,1024]{1,0:T(8,128)(2,1)}, bf16[256,1024]{1,0:T(8,128)(2,1)}, f32[256,1024]{1,0:T(8,128)}, bf16[272...) custom-call(bf16[256,1024]{1,0:T(8,128)(2,1)} %get-tuple-element.68.dq, f32[256,2048]{1,0:T(8,128)} %get-tuple-element.69.dkv, ...), custom_call_target="tpu_custom_call" | custom-call | flops 3758096384 | bytes 4000000 | tf_op jit(solution)/shard_map/pallas_call | solution.py:65
  187.7 7.0 %collective-permute-done.22.r_3_ = bf16[272,256]{1,0:T(8,128)(2,1)S(1)} collective-permute-done((bf16[272,256]{1,0:T(8,128)(2,1)}, bf16[272,256]{1,0:T(8,128)(2,1)S(1)}, u32[]{:S(2)}, u32[]{:S(2)}) %collective-permute-start.22) | collective-permute-done | bytes 139296 | tf_op jit(solution)/shard_map/ppermute | solution.py:446
  196.9 21.3 %shard_map.328 = (bf16[4,2048,261]{2,1,0:T(8,128)(2,1)}, bf16[4,272,256]{2,1,0:T(8,128)(2,1)}, bf16[4,272,256]{2,1,0:T(8,128)(2,1)}) custom-call(s32[5]{0:T(128)} %stack.23.r_0_.pos, bf16[272,256]{1,0:T(8,128)(2,1)} %get-tuple-element.77.r_1_, bf16[272,256]{1,0:T(8,128)(2,1)} %copy-done.23, bf16[272,256]{1,0:T(8,128)(2,1)} %copy-done.24, ...), custom_call_target="tpu_custom_call" | custom-call | flops 17179869184 | bytes 12582912 | tf_op jit(solution)/shard_map/pallas_call | solution.py:643
  225.9 6.0 %all-to-all-done.6 = bf16[8,272,128]{2,1,0:T(8,128)(2,1)} async-done(((bf16[8,272,128]{2,1,0:T(8,128)(2,1)}), bf16[8,272,128]{2,1,0:T(8,128)(2,1)}, u32[]{:S(2)}, u32[]{:S(2)}) %all-to-all-start.6) | async-done | bytes 557088 | tf_op jit(solution)/shard_map/all_to_all | solution.py:459
  241.4 14.5 %all-to-all-done.11 = bf16[2,128,3072]{2,1,0:T(8,128)(2,1)} async-done(((bf16[2,128,3072]{2,1,0:T(8,128)(2,1)}), bf16[2,128,3072]{2,1,0:T(8,128)(2,1)}, u32[]{:S(2)}, u32[]{:S(2)}) %all-to-all-start.11) | async-done | bytes 1572896 | tf_op jit(solution)/shard_map/all_to_all | solution.py:488
  264.9 9.7 %all-to-all-done.3 = bf16[4,272,256]{2,1,0:T(8,128)(2,1)} async-done(((bf16[4,272,256]{2,1,0:T(8,128)(2,1)}), bf16[4,272,256]{2,1,0:T(8,128)(2,1)}, u32[]{:S(2)}, u32[]{:S(2)}) %all-to-all-start.3) | async-done | bytes 557088 | tf_op jit(solution)/shard_map/all_to_all | solution.py:606
  297.5 4.9 %all-to-all-done.4 = bf16[4,32,1024]{2,1,0:T(8,128)(2,1)S(1)} async-done(((bf16[4,32,1024]{2,1,0:T(8,128)(2,1)}), bf16[4,32,1024]{2,1,0:T(8,128)(2,1)S(1)}, u32[]{:S(2)}, u32[]{:S(2)}) %all-to-all-start.4) | async-done | bytes 262176 | tf_op jit(solution)/shard_map/all_to_all | solution.py:687
  309.8 6.0 %all-to-all-done.5 = bf16[8,272,128]{2,1,0:T(8,128)(2,1)} async-done(((bf16[8,272,128]{2,1,0:T(8,128)(2,1)}), bf16[8,272,128]{2,1,0:T(8,128)(2,1)}, u32[]{:S(2)}, u32[]{:S(2)}) %all-to-all-start.5) | async-done | bytes 557088 | tf_op jit(solution)/shard_map/all_to_all | solution.py:459
  321.9 16.9 %all-to-all-done.9 = bf16[2,128,3072]{2,1,0:T(8,128)(2,1)S(1)} async-done(((bf16[2,128,3072]{2,1,0:T(8,128)(2,1)}), bf16[2,128,3072]{2,1,0:T(8,128)(2,1)S(1)}, u32[]{:S(2)}, u32[]{:S(2)}) %all-to-all-start.9) | async-done | bytes 1572896 | tf_op jit(solution)/shard_map/all_to_all | solution.py:488
  345.1 10.8 %all-to-all-done.8 = bf16[4,32,2048]{2,1,0:T(8,128)(2,1)S(1)} async-done(((bf16[4,32,2048]{2,1,0:T(8,128)(2,1)}), bf16[4,32,2048]{2,1,0:T(8,128)(2,1)S(1)}, u32[]{:S(2)}, u32[]{:S(2)}) %all-to-all-start.8) | async-done | bytes 524320 | tf_op jit(solution)/shard_map/all_to_all | solution.py:490
  359.4 10.8 %copy.90 = bf16[4,2048,261]{1,0,2:T(4,128)(2,1)} copy(bf16[4,2048,261]{2,1,0:T(8,128)(2,1)} %get-tuple-element.162) | data formatting | bytes 8552448
  371.4 15.4 %all-gather.2 = bf16[1088,128]{1,0:T(8,128)(2,1)S(1)} all-gather(bf16[272,128]{1,0:T(8,128)(2,1)S(1)} %reduce_sum.139), channel_id=4, replica_groups=mesh['item'=2,'lat'=4,'pix'=4] {'pix'}, dimensions={0}, use_global_device_ids=true | all-gather | bytes 348160 | tf_op jit(solution)/shard_map/all_gather | solution.py:461
  386.8 10.0 %all-gather.3 = bf16[2176,128]{1,0:T(8,128)(2,1)S(1)} all-gather(bf16[272,128]{1,0:T(8,128)(2,1)S(1)} %reduce_sum.140), channel_id=5, replica_groups=mesh['item'=2,'lat'=4,'pix'=4] {'item','lat'}, dimensions={0}, use_global_device_ids=true | all-gather | bytes 626688 | tf_op jit(solution)/shard_map/all_gather | solution.py:462
  409.9 26.3 %all-gather = bf16[1088,128]{1,0:T(8,128)(2,1)S(1)} all-gather(bf16[272,128]{1,0:T(8,128)(2,1)S(1)} %reduce_sum.137), channel_id=2, replica_groups=mesh['item'=2,'lat'=4,'pix'=4] {'pix'}, dimensions={0}, use_global_device_ids=true | all-gather | bytes 348160 | tf_op jit(solution)/shard_map/all_gather | solution.py:461
  436.3 9.1 %all-gather.1 = bf16[2176,128]{1,0:T(8,128)(2,1)S(1)} all-gather(bf16[272,128]{1,0:T(8,128)(2,1)S(1)} %reduce_sum.138), channel_id=3, replica_groups=mesh['item'=2,'lat'=4,'pix'=4] {'item','lat'}, dimensions={0}, use_global_device_ids=true | all-gather | bytes 626688 | tf_op jit(solution)/shard_map/all_gather | solution.py:462
  (238 shorter events, 171.1 us)
Async XLA Ops:
  13.5 17.3 %collective-permute-start.8 = (bf16[272,128]{1,0:T(8,128)(2,1)S(1)}, bf16[272,128]{1,0:T(8,128)(2,1)S(1)}, u32[]{:S(2)}, u32[]{:S(2)}) collective-permute-start(bf16[272,128]{1,0:T(8,128)(2,1)S(1)} %collective-permute-done.r_2_), channel_id=1, source_target_pairs={{0,8},{4,12},{8,0},{12,4},{1,9},{5,13},{9,1},{13,5},{2,10},{6,14},... | collective-permute-start | bytes 208904 | tf_op jit(solution)/shard_map/ppermute | solution.py:440
  17.6 14.0 %collective-permute-start.4 = (bf16[272,128]{1,0:T(8,128)(2,1)S(1)}, bf16[272,128]{1,0:T(8,128)(2,1)S(1)}, u32[]{:S(2)}, u32[]{:S(2)}) collective-permute-start(bf16[272,128]{1,0:T(8,128)(2,1)S(1)} %collective-permute-done.r_2_), channel_id=1, source_target_pairs={{0,4},{4,0},{8,12},{12,8},{1,5},{5,1},{9,13},{13,9},{2,6},{6,2},{1... | collective-permute-start | bytes 208904 | tf_op jit(solution)/shard_map/ppermute | solution.py:440
  17.6 13.4 %collective-permute-start.9 = (bf16[272,128]{1,0:T(8,128)(2,1)S(1)}, bf16[272,128]{1,0:T(8,128)(2,1)S(1)}, u32[]{:S(2)}, u32[]{:S(2)}) collective-permute-start(bf16[272,128]{1,0:T(8,128)(2,1)S(1)} %collective-permute-done.1.r_3_), channel_id=1, source_target_pairs={{0,8},{4,12},{8,0},{12,4},{1,9},{5,13},{9,1},{13,5},{2,10},{6,14},... | collective-permute-start | bytes 208904 | tf_op jit(solution)/shard_map/ppermute | solution.py:440
  19.2 12.8 %collective-permute-start.5 = (bf16[272,128]{1,0:T(8,128)(2,1)S(1)}, bf16[272,128]{1,0:T(8,128)(2,1)S(1)}, u32[]{:S(2)}, u32[]{:S(2)}) collective-permute-start(bf16[272,128]{1,0:T(8,128)(2,1)S(1)} %collective-permute-done.1.r_3_), channel_id=1, source_target_pairs={{0,4},{4,0},{8,12},{12,8},{1,5},{5,1},{9,13},{13,9},{2,6},{6,2},{1... | collective-permute-start | bytes 208904 | tf_op jit(solution)/shard_map/ppermute | solution.py:440
  19.4 12.2 %collective-permute-start.10 = (bf16[272,128]{1,0:T(8,128)(2,1)S(1)}, bf16[272,128]{1,0:T(8,128)(2,1)S(1)}, u32[]{:S(2)}, u32[]{:S(2)}) collective-permute-start(bf16[272,128]{1,0:T(8,128)(2,1)S(1)} %collective-permute-done.2.r_4_), channel_id=1, source_target_pairs={{0,8},{4,12},{8,0},{12,4},{1,9},{5,13},{9,1},{13,5},{2,10},{6,14},... | collective-permute-start | bytes 208904 | tf_op jit(solution)/shard_map/ppermute | solution.py:440
  60.5 18.5 %all-to-all-start.1 = ((bf16[4,64,1024]{2,1,0:T(8,128)(2,1)}), bf16[4,64,1024]{2,1,0:T(8,128)(2,1)S(1)}, u32[]{:S(2)}, u32[]{:S(2)}) async-start(bf16[4,64,1024]{2,1,0:T(8,128)(2,1)} %pad_maximum_fusion.2), calls=%async_computation.1 | async-start | bytes 1048576 | tf_op jit(solution)/shard_map/all_to_all | solution.py:566
  79.0 18.6 %all-to-all-start = ((bf16[4,272,256]{2,1,0:T(8,128)(2,1)}), bf16[4,272,256]{2,1,0:T(8,128)(2,1)S(1)}, u32[]{:S(2)}, u32[]{:S(2)}) async-start(bf16[4,272,256]{2,1,0:T(8,128)(2,1)} %add_convert_fusion.1), calls=%async_computation | async-start | bytes 1114112 | tf_op jit(solution)/shard_map/all_to_all | solution.py:606
  82.9 16.5 %collective-permute-start.17 = (bf16[128,1024]{1,0:T(8,128)(2,1)S(1)}, bf16[128,1024]{1,0:T(8,128)(2,1)S(1)}, u32[]{:S(2)}, u32[]{:S(2)}) collective-permute-start(bf16[128,1024]{1,0:T(8,128)(2,1)S(1)} %bitcast.94), channel_id=1, source_target_pairs={{0,8},{4,12},{8,0},{12,4},{1,9},{5,13},{9,1},{13,5},{2,10},{6,14},... | collective-permute-start | bytes 786440 | tf_op jit(solution)/shard_map/ppermute | solution.py:440
  114.3 15.0 %collective-permute-start.18 = (bf16[256,2048]{1,0:T(8,128)(2,1)}, bf16[256,2048]{1,0:T(8,128)(2,1)}, u32[]{:S(2)}, u32[]{:S(2)}) collective-permute-start(bf16[256,2048]{1,0:T(8,128)(2,1)} %get-tuple-element.65.kv), channel_id=1, source_target_pairs={{0,4},{4,0},{8,12},{12,8},{1,5},{5,1},{9,13},{13,9},{2,6},{6,2},{1... | collective-permute-start | bytes 3145736 | tf_op jit(solution)/shard_map/ppermute | solution.py:440
  157.9 64.9 %collective-permute-start.32 = (bf16[2,128,3072]{2,1,0:T(8,128)(2,1)}, bf16[2,128,3072]{2,1,0:T(8,128)(2,1)}, u32[]{:S(2)}, u32[]{:S(2)}) collective-permute-start(bf16[2,128,3072]{2,1,0:T(8,128)(2,1)} %dynamic-slice_bitcast_fusion), channel_id=1, source_target_pairs={{0,4},{4,0},{8,12},{12,8},{1,5},{5,1},{9,13},{13,9},{2,6},{6,2},{1... | collective-permute-start | bytes 4718600 | tf_op jit(solution)/shard_map/ppermute | solution.py:440
  161.2 57.3 %all-to-all-start.2 = ((bf16[4,32,1024]{2,1,0:T(8,128)(2,1)}), bf16[4,32,1024]{2,1,0:T(8,128)(2,1)}, u32[]{:S(2)}, u32[]{:S(2)}) async-start(bf16[4,32,1024]{2,1,0:T(8,128)(2,1)} %bitcast.109), calls=%async_computation.2 | async-start | bytes 524288 | tf_op jit(solution)/shard_map/all_to_all | solution.py:687
  183.7 12.4 %collective-permute-start.24 = (bf16[272,256]{1,0:T(8,128)(2,1)}, bf16[272,256]{1,0:T(8,128)(2,1)S(1)}, u32[]{:S(2)}, u32[]{:S(2)}) collective-permute-start(bf16[272,256]{1,0:T(8,128)(2,1)} %get-tuple-element.77.r_1_), channel_id=1, source_target_pairs={{0,4},{4,0},{8,12},{12,8},{1,5},{5,1},{9,13},{13,9},{2,6},{6,2},{1... | collective-permute-start | bytes 417800 | tf_op jit(solution)/shard_map/ppermute | solution.py:440
  218.2 21.1 %collective-permute-start.28 = (bf16[4,272,256]{2,1,0:T(8,128)(2,1)}, bf16[4,272,256]{2,1,0:T(8,128)(2,1)}, u32[]{:S(2)}, u32[]{:S(2)}) collective-permute-start(bf16[4,272,256]{2,1,0:T(8,128)(2,1)} %get-tuple-element.81), channel_id=1, source_target_pairs={{0,4},{4,0},{8,12},{12,8},{1,5},{5,1},{9,13},{13,9},{2,6},{6,2},{1... | collective-permute-start | bytes 1671176 | tf_op jit(solution)/shard_map/ppermute | solution.py:440
  218.5 13.4 %all-to-all-start.6 = ((bf16[8,272,128]{2,1,0:T(8,128)(2,1)}), bf16[8,272,128]{2,1,0:T(8,128)(2,1)}, u32[]{:S(2)}, u32[]{:S(2)}) async-start(bf16[8,272,128]{2,1,0:T(8,128)(2,1)} %bitcast_bitcast_fusion), calls=%async_computation.6 | async-start | bytes 1114112 | tf_op jit(solution)/shard_map/all_to_all | solution.py:459
  231.9 24.0 %all-to-all-start.11 = ((bf16[2,128,3072]{2,1,0:T(8,128)(2,1)}), bf16[2,128,3072]{2,1,0:T(8,128)(2,1)}, u32[]{:S(2)}, u32[]{:S(2)}) async-start(bf16[2,128,3072]{2,1,0:T(8,128)(2,1)} %fusion), calls=%async_computation.11 | async-start | bytes 3145728 | tf_op jit(solution)/shard_map/all_to_all | solution.py:488
  237.6 23.8 %collective-permute-start.30 = (bf16[2,128,2048]{2,1,0:T(8,128)(2,1)}, bf16[2,128,2048]{2,1,0:T(8,128)(2,1)}, u32[]{:S(2)}, u32[]{:S(2)}) collective-permute-start(bf16[2,128,2048]{2,1,0:T(8,128)(2,1)} %dynamic-slice_bitcast_fusion.2), channel_id=1, source_target_pairs={{0,4},{4,0},{8,12},{12,8},{1,5},{5,1},{9,13},{13,9},{2,6},{6,2},{1... | collective-permute-start | bytes 3145736 | tf_op jit(solution)/shard_map/ppermute | solution.py:440
  255.9 18.6 %all-to-all-start.3 = ((bf16[4,272,256]{2,1,0:T(8,128)(2,1)}), bf16[4,272,256]{2,1,0:T(8,128)(2,1)}, u32[]{:S(2)}, u32[]{:S(2)}) async-start(bf16[4,272,256]{2,1,0:T(8,128)(2,1)} %add_convert_fusion), calls=%async_computation.3 | async-start | bytes 1114112 | tf_op jit(solution)/shard_map/all_to_all | solution.py:606
  261.4 45.3 %collective-permute-start.31 = (bf16[2,128,3072]{2,1,0:T(8,128)(2,1)}, bf16[2,128,3072]{2,1,0:T(8,128)(2,1)}, u32[]{:S(2)}, u32[]{:S(2)}) collective-permute-start(bf16[2,128,3072]{2,1,0:T(8,128)(2,1)} %dynamic-slice_bitcast_fusion.1), channel_id=1, source_target_pairs={{0,4},{4,0},{8,12},{12,8},{1,5},{5,1},{9,13},{13,9},{2,6},{6,2},{1... | collective-permute-start | bytes 4718600 | tf_op jit(solution)/shard_map/ppermute | solution.py:440
  274.5 17.6 %all-to-all-start.7 = ((bf16[2,128,2048]{2,1,0:T(8,128)(2,1)}), bf16[2,128,2048]{2,1,0:T(8,128)(2,1)}, u32[]{:S(2)}, u32[]{:S(2)}) async-start(bf16[2,128,2048]{2,1,0:T(8,128)(2,1)} %fusion.2), calls=%async_computation.7 | async-start | bytes 2097152 | tf_op jit(solution)/shard_map/all_to_all | solution.py:488
  302.4 13.4 %all-to-all-start.5 = ((bf16[8,272,128]{2,1,0:T(8,128)(2,1)}), bf16[8,272,128]{2,1,0:T(8,128)(2,1)}, u32[]{:S(2)}, u32[]{:S(2)}) async-start(bf16[8,272,128]{2,1,0:T(8,128)(2,1)} %bitcast_bitcast_fusion.1), calls=%async_computation.5 | async-start | bytes 1114112 | tf_op jit(solution)/shard_map/all_to_all | solution.py:459
  315.8 23.0 %all-to-all-start.9 = ((bf16[2,128,3072]{2,1,0:T(8,128)(2,1)}), bf16[2,128,3072]{2,1,0:T(8,128)(2,1)S(1)}, u32[]{:S(2)}, u32[]{:S(2)}) async-start(bf16[2,128,3072]{2,1,0:T(8,128)(2,1)} %fusion.1), calls=%async_computation.9 | async-start | bytes 3145728 | tf_op jit(solution)/shard_map/all_to_all | solution.py:488
  338.8 17.1 %all-to-all-start.8 = ((bf16[4,32,2048]{2,1,0:T(8,128)(2,1)}), bf16[4,32,2048]{2,1,0:T(8,128)(2,1)S(1)}, u32[]{:S(2)}, u32[]{:S(2)}) async-start(bf16[4,32,2048]{2,1,0:T(8,128)(2,1)} %bitcast.27), calls=%async_computation.8 | async-start | bytes 1048576 | tf_op jit(solution)/shard_map/all_to_all | solution.py:490
  355.9 47.5 %all-to-all-start.12 = ((bf16[4,32,3072]{2,1,0:T(8,128)(2,1)}), bf16[4,32,3072]{2,1,0:T(8,128)(2,1)S(1)}, u32[]{:S(2)}, u32[]{:S(2)}) async-start(bf16[4,32,3072]{2,1,0:T(8,128)(2,1)} %bitcast.39), calls=%async_computation.12 | async-start | bytes 1572864 | tf_op jit(solution)/shard_map/all_to_all | solution.py:490
  403.4 50.4 %all-to-all-start.10 = ((bf16[4,32,3072]{2,1,0:T(8,128)(2,1)}), bf16[4,32,3072]{2,1,0:T(8,128)(2,1)S(1)}, u32[]{:S(2)}, u32[]{:S(2)}) async-start(bf16[4,32,3072]{2,1,0:T(8,128)(2,1)} %bitcast.32), calls=%async_computation.10 | async-start | bytes 1572864 | tf_op jit(solution)/shard_map/all_to_all | solution.py:490
  (68 other events, 553.3 us)
